TPU v7x, 512 devices: a whole 4x8x8 slice. The times are simulated.
512 devices in a mesh: row: 32 (over x, y), col: 16 (over z, core).
Axes of the slice: x: 4, y: 8, z: 8, core: 2. Of those that a mesh axis runs over, the one named last changes fastest.
Arguments:
- matrix: float32 [1, 4096, 2, 2048], P(None, 'row', None, 'col'), may hold values from 0 to 2, as said below
Outputs:
- factored: float32 [1, 4096, 2, 2048], P(None, 'row', None, 'col')
Inputs may be any that keep to these rules, and one draw needn't show every extreme that they name: `matrix`: symmetric and positive definite, with every eigenvalue at least 1.
All inputs are finite; a program needn't handle non-finite values.
Results may differ from a plain program's by a relative error of at most 0.0003.
Values sent between devices are 32-bit elements; how exact they have to be, the bound alone decides.
No kernel may reach another device: no remote copies, remote signals or barrier semaphores. Data moves between devices by JAX's collectives and lax.ppermute only.
A program may use at most 64 MiB of HBM per device.

v0:
```python
import jax
import jax.numpy as jnp
from jax import lax
from jax.sharding import PartitionSpec as P

PANEL = 384


def from_root(array, axis, root):
    mine = lax.axis_index(axis) == root
    return lax.psum(jnp.where(mine, array, jnp.zeros_like(array)), axis)


def global_index(tile_count, tile_size, stride, position):
    within = jnp.arange(tile_count * tile_size, dtype=jnp.int32)
    return (within // tile_size * stride + position) * tile_size + within % tile_size


def transpose_tiles(lower_part, tile_size, tile_cols):
    row_count = lax.axis_size("row")
    col_count = lax.axis_size("col")
    col_position = lax.axis_index("col")
    panel_width = lower_part.shape[1]

    def receive_tile(column_tile, buffer):
        global_tile = column_tile * col_count + col_position
        arrived = from_root(lower_part, "row", global_tile % row_count)
        return lax.dynamic_update_slice_in_dim(buffer, arrived, column_tile * tile_size, 0)

    initial = jnp.zeros((tile_cols * tile_size, panel_width), jnp.float32)
    return lax.fori_loop(0, tile_cols, receive_tile, initial)


def factor_panel(local_block, panel_start, panel_width, tile_size, global_rows, global_cols):
    row_count = lax.axis_size("row")
    col_count = lax.axis_size("col")
    col_position = lax.axis_index("col")
    first_tile = panel_start // tile_size
    tile_count = panel_width // tile_size
    pieces = []
    for member in range(tile_count):
        global_tile = first_tile + member
        local_tile = global_tile // col_count
        tile_piece = local_block[:, local_tile * tile_size : (local_tile + 1) * tile_size]
        pieces.append(from_root(tile_piece, "col", global_tile % col_count))
    panel_cols = jnp.concatenate(pieces, axis=1)
    strips = []
    for member in range(tile_count):
        global_tile = first_tile + member
        local_tile = global_tile // row_count
        strips.append(from_root(panel_cols, "row", global_tile % row_count))
    diag_block = jnp.concatenate(strips, axis=0)
    factor = jnp.linalg.cholesky(diag_block)
    identity = jnp.eye(panel_width, dtype=jnp.float32)
    inverse = jax.scipy.linalg.solve_triangular(factor, identity, lower=True)
    product = jnp.dot(
        panel_cols, inverse.T, precision=lax.Precision.HIGHEST, preferred_element_type=jnp.float32
    )
    panel_index = panel_start + jnp.arange(panel_width, dtype=jnp.int32)
    lower_part = jnp.where(global_rows[:, None] >= panel_index[None, :], product, 0.0)
    column_side = transpose_tiles(lower_part, tile_size, global_cols.shape[0] // tile_size)
    update = jnp.dot(
        lower_part,
        column_side.T,
        precision=lax.Precision.HIGHEST,
        preferred_element_type=jnp.float32,
    )
    panel_end = panel_start + panel_width
    later_rows = global_rows >= panel_end
    later_cols = global_cols >= panel_end
    inside_rows = (global_rows >= panel_start) & (global_rows < panel_end)
    result = jnp.where(later_rows[:, None] & later_cols[None, :], local_block - update, local_block)
    result = jnp.where(inside_rows[:, None] & later_cols[None, :], 0.0, result)
    for member in range(tile_count):
        global_tile = first_tile + member
        local_tile = global_tile // col_count
        is_owner = col_position == global_tile % col_count
        current = result[:, local_tile * tile_size : (local_tile + 1) * tile_size]
        replaced = jnp.where(
            is_owner, lower_part[:, member * tile_size : (member + 1) * tile_size], current
        )
        result = result.at[:, local_tile * tile_size : (local_tile + 1) * tile_size].set(replaced)
    return result


def per_device(matrix):
    tile_rows = matrix.shape[0]
    tile_size = matrix.shape[1]
    tile_cols = matrix.shape[2]
    row_count = lax.axis_size("row")
    col_count = lax.axis_size("col")
    local_block = matrix.reshape(tile_rows * tile_size, tile_cols * tile_size)
    global_rows = global_index(tile_rows, tile_size, row_count, lax.axis_index("row"))
    global_cols = global_index(tile_cols, tile_size, col_count, lax.axis_index("col"))
    panel_spans = ((0, PANEL), (PANEL, PANEL))
    for panel_start, panel_width in panel_spans:
        local_block = factor_panel(
            local_block, panel_start, panel_width, tile_size, global_rows, global_cols
        )
    return local_block.reshape(matrix.shape)


def solution(mesh):
    placed = (P(None, "row", None, "col"),)
    return jax.shard_map(
        per_device,
        mesh=mesh,
        in_specs=placed,
        out_specs=P(None, "row", None, "col"),
        check_vma=False,
    )
```

profile of v0, /device:TPU:1, one launch (start us, length us, event | category | flops | bytes accessed | tf_op | source)
XLA Modules:
  0.0 1396.1 jit_solution(10206552368104848708)
XLA Ops:
  6.5 1.0 copy.2
  8.3 118.4 %all-reduce.18.cloned.1.call-done = (f32[128,128]{0,1:T(8,128)}, f32[128,128]{0,1:T(8,128)}, f32[128,128]{0,1:T(8,128)}) async-done(((f32[128,128]{0,1:T(8,128)}, f32[128,128]{0,1:T(8,128)}, f32[128,128]{0,1:T(8,128)}), (f32[128,128]{0,1:T(8,128)}, f32[128,128]{0,1:T(8,128)}, f32[128,128]{0,1:T(8,128)})) %all-reduce.18.cloned.1.call-update) | async-done | bytes 196624 | tf_op jit(solution)/shard_map/psum | solution.py:11
  130.1 154.3 %all-reduce.14.cloned.1.call-done = (f32[128,384]{0,1:T(8,128)}, f32[128,384]{0,1:T(8,128)}, f32[128,384]{0,1:T(8,128)}) async-done(((f32[128,384]{0,1:T(8,128)}, f32[128,384]{0,1:T(8,128)}, f32[128,384]{0,1:T(8,128)}), (f32[128,384]{0,1:T(8,128)}, f32[128,384]{0,1:T(8,128)}, f32[128,384]{0,1:T(8,128)})) %all-reduce.14.cloned.1.call-update) | async-done | bytes 589840 | tf_op jit(solution)/shard_map/psum | solution.py:11
  286.6 11.7 cholesky.208
  298.4 9.8 custom-call.20
  308.8 11.7 cholesky.227
  320.6 10.0 custom-call.21
  331.0 11.7 cholesky.246
  346.0 5.8 while.42
  346.6 1.3 bitcast_dynamic-update-slice_fusion.4
  348.6 1.3 bitcast_dynamic-update-slice_fusion.4
  350.5 1.3 bitcast_dynamic-update-slice_fusion.4
  351.8 29.5 %custom-call.22 = f32[3,128,128]{1,2,0:T(8,128)S(1)} custom-call(f32[3,128,128]{2,1,0:T(8,128)S(1)} %get-tuple-element.317), custom_call_target="InvertDiagBlocksLowerTriangular" | custom-call | tf_op jit(solution)/shard_map/jit(_solve_triangular)/triangular_solve | solution.py:55
  383.9 313.1 %while.40 = (s32[]{:T(128)}, f32[256,384]{1,0:T(8,128)S(1)}, s32[]{:T(128)}, f32[128,384]{1,0:T(8,128)S(1)}, s32[]{:T(128)}, /*index=5*/u32[]{:T(128)}, u32[]{:T...) while((s32[]{:T(128)}, f32[256,384]{1,0:T(8,128)S(1)}, ...), condition=%wide.region_14.17_spmd, body=%wide.region_12.16_spmd.sunk | while | flops 98327 | bytes 1966470 | solution.py:31
  384.8 154.8 %all-reduce.20.cloned.1.call-done = f32[128,384]{1,0:T(8,128)} async-done(((f32[128,384]{1,0:T(8,128)}), f32[128,384]{1,0:T(8,128)}) %all-reduce.20.cloned.1.call-update) | async-done | bytes 196624 | tf_op jit(solution)/shard_map/while/body/eval_jaxpr/psum | solution.py:11
  541.4 154.7 %all-reduce.20.cloned.1.call-done = f32[128,384]{1,0:T(8,128)} async-done(((f32[128,384]{1,0:T(8,128)}), f32[128,384]{1,0:T(8,128)}) %all-reduce.20.cloned.1.call-update) | async-done | bytes 196624 | tf_op jit(solution)/shard_map/while/body/eval_jaxpr/psum | solution.py:11
  697.6 1.3 broadcast_select_fusion.8
  700.4 113.3 %all-reduce.16.cloned.1.call-done = (f32[128,128]{0,1:T(8,128)}, f32[128,128]{0,1:T(8,128)}, f32[128,128]{0,1:T(8,128)}) async-done(((f32[128,128]{0,1:T(8,128)}, f32[128,128]{0,1:T(8,128)}, f32[128,128]{0,1:T(8,128)}), (f32[128,128]{0,1:T(8,128)}, f32[128,128]{0,1:T(8,128)}, f32[128,128]{0,1:T(8,128)})) %all-reduce.16.cloned.1.call-update) | async-done | bytes 196624 | tf_op jit(solution)/shard_map/psum | solution.py:11
  816.3 154.9 %all-reduce.12.cloned.1.call-done = (f32[128,384]{0,1:T(8,128)}, f32[128,384]{0,1:T(8,128)}, f32[128,384]{0,1:T(8,128)}) async-done(((f32[128,384]{0,1:T(8,128)}, f32[128,384]{0,1:T(8,128)}, f32[128,384]{0,1:T(8,128)}), (f32[128,384]{0,1:T(8,128)}, f32[128,384]{0,1:T(8,128)}, f32[128,384]{0,1:T(8,128)})) %all-reduce.12.cloned.1.call-update) | async-done | bytes 589840 | tf_op jit(solution)/shard_map/psum | solution.py:11
  973.5 11.7 cholesky.261
  985.3 9.8 custom-call.23
  995.7 11.7 cholesky.280
  1008.7 10.0 custom-call.24
  1019.3 11.7 cholesky.299
  1033.6 5.8 while.43
  1034.2 1.3 bitcast_dynamic-update-slice_fusion.5
  1036.2 1.3 bitcast_dynamic-update-slice_fusion.5
  1038.1 1.3 bitcast_dynamic-update-slice_fusion.5
  1039.4 29.5 %custom-call.25 = f32[3,128,128]{1,2,0:T(8,128)S(1)} custom-call(f32[3,128,128]{2,1,0:T(8,128)S(1)} %get-tuple-element.318), custom_call_target="InvertDiagBlocksLowerTriangular" | custom-call | tf_op jit(solution)/shard_map/jit(_solve_triangular)/triangular_solve | solution.py:55
  1071.5 314.1 %while.41 = (s32[]{:T(128)}, f32[256,384]{1,0:T(8,128)S(1)}, s32[]{:T(128)}, f32[128,384]{1,0:T(8,128)S(1)}, s32[]{:T(128)}, /*index=5*/u32[]{:T(128)}, u32[]{:T...) while((s32[]{:T(128)}, f32[256,384]{1,0:T(8,128)S(1)}, ...), condition=%wide.region_24.27_spmd, body=%wide.region_22.26_spmd.sunk | while | flops 98327 | bytes 1966470 | solution.py:31
  1072.4 155.2 %all-reduce.22.cloned.1.call-done = f32[128,384]{1,0:T(8,128)} async-done(((f32[128,384]{1,0:T(8,128)}), f32[128,384]{1,0:T(8,128)}) %all-reduce.22.cloned.1.call-update) | async-done | bytes 196624 | tf_op jit(solution)/shard_map/while/body/eval_jaxpr/psum | solution.py:11
  1229.3 155.4 %all-reduce.22.cloned.1.call-done = f32[128,384]{1,0:T(8,128)} async-done(((f32[128,384]{1,0:T(8,128)}), f32[128,384]{1,0:T(8,128)}) %all-reduce.22.cloned.1.call-update) | async-done | bytes 196624 | tf_op jit(solution)/shard_map/while/body/eval_jaxpr/psum | solution.py:11
  (135 shorter events, 37.8 us)
Async XLA Ops:
  6.5 120.2 %all-reduce.18.cloned.1.call-start = ((), (), s32[]{:S(2)}) async-start(), calls=%async_computation.3 | async-start | bytes 393216 | tf_op jit(solution)/shard_map/psum | solution.py:11
  8.2 276.1 %all-reduce.14.cloned.1.call-start = ((), (), s32[]{:S(2)}) async-start(), calls=%async_computation.1 | async-start | bytes 1179648 | tf_op jit(solution)/shard_map/psum | solution.py:11
  126.7 0.9 copy-start.5
  127.6 0.8 copy-start.4
  284.3 1.0 copy-start.1
  285.4 0.9 copy-start
  383.9 155.7 %all-reduce.20.cloned.1.call-start = ((), (), s32[]{:S(2)}) async-start(), calls=%async_computation.4 | async-start | bytes 393216 | tf_op jit(solution)/shard_map/while/body/eval_jaxpr/psum | solution.py:11
  540.6 155.5 %all-reduce.20.cloned.1.call-start = ((), (), s32[]{:S(2)}) async-start(), calls=%async_computation.4 | async-start | bytes 393216 | tf_op jit(solution)/shard_map/while/body/eval_jaxpr/psum | solution.py:11
  697.0 116.6 %all-reduce.16.cloned.1.call-start = ((), (), s32[]{:S(2)}) async-start(), calls=%async_computation.2 | async-start | bytes 393216 | tf_op jit(solution)/shard_map/psum | solution.py:11
  700.1 271.1 %all-reduce.12.cloned.1.call-start = ((), (), s32[]{:S(2)}) async-start(), calls=%async_computation | async-start | bytes 1179648 | tf_op jit(solution)/shard_map/psum | solution.py:11
  813.7 0.9 copy-start.7
  814.6 0.8 copy-start.6
  971.2 1.0 copy-start.3
  972.2 0.9 copy-start.2
  1071.5 156.0 %all-reduce.22.cloned.1.call-start = ((), (), s32[]{:S(2)}) async-start(), calls=%async_computation.5 | async-start | bytes 393216 | tf_op jit(solution)/shard_map/while/body/eval_jaxpr/psum | solution.py:11
  1228.5 156.2 %all-reduce.22.cloned.1.call-start = ((), (), s32[]{:S(2)}) async-start(), calls=%async_computation.5 | async-start | bytes 393216 | tf_op jit(solution)/shard_map/while/body/eval_jaxpr/psum | solution.py:11
Sparse Core Ops, SparseCore 0:
  9.9 116.7 all-reduce.17
  130.7 153.5 all-reduce.13
  388.2 151.3 all-reduce.19
  544.5 151.5 all-reduce.19
  700.3 113.3 all-reduce.15
  817.6 153.5 all-reduce.11
  1076.2 151.3 all-reduce.21
  1233.2 151.5 all-reduce.21
where the time goes:
time: 1410 us; the launch traced here: 1400 us
  waiting for transfers between devices  1160 us (82%)
  other arithmetic  183 us (13%)
  local copies, waits for them, and re-layouts  25.2 us (2%)
  between operations  18 us (1%)
    psum x8, waiting for transfers between devices, from_root(): return lax.psum(jnp.where(mine, array, jnp.zeros_like(array)), axis)  1160 us
    another operation x21, other arithmetic, factor_panel(): factor = jnp.linalg.cholesky(diag_block)  113 us
    another operation x5, other arithmetic, factor_panel(): inverse = jax.scipy.linalg.solve_triangular(factor, identity, lower=True)  59.1 us
  transfers between devices with their start and end apart: 8, of which 8 were waited for; matrix products, arithmetic and copies ran while one was open for 0% of the time, Pallas kernels for 0%

commit v1 on v0

v1 whole, which is shorter than its diff:
```python
import jax
import jax.numpy as jnp
from jax import lax
from jax.experimental import pallas as pl
from jax.experimental.pallas import tpu as pltpu
from jax.sharding import PartitionSpec as P

TILE = 128
NB = 6
GROUP = 32
XS, YS, ZS = 4, 8, 8
ZSRC = NB // 2
PAYLOAD = 5
VMEM_LIMIT = 48 * 1024 * 1024
HI = lax.Precision.HIGHEST


def dot(a, b):
    return lax.dot_general(a, b, (((1,), (0,)), ((), ())), precision=HI, preferred_element_type=jnp.float32)


def dot_t(a, b):
    return lax.dot_general(a, b, (((0,), (0,)), ((), ())), precision=HI, preferred_element_type=jnp.float32)


def spread(row):
    return jnp.broadcast_to(row, (8, row.shape[1]))


def eliminate(rows, offset):
    count, width = rows.shape
    groups = count // 8
    wide = width // TILE
    block = rows[:, offset : offset + count]
    column = {}
    for j in range(count):
        for g in range(j // 8, groups):
            column[g, j] = jnp.broadcast_to(block[8 * g : 8 * g + 8, j : j + 1], (8, TILE))
    part = [rows[8 * g : 8 * g + 8] for g in range(groups)]
    sublane = lax.broadcasted_iota(jnp.int32, (8, TILE), 0)
    scale = [None] * groups
    for k in range(count):
        gk, sk = divmod(k, 8)
        pivot = spread(column[gk, k][sk : sk + 1])
        inverse = pl.reciprocal(pivot)
        root = lax.rsqrt(pivot)
        scale[gk] = root if scale[gk] is None else jnp.where(sublane == sk, root, scale[gk])
        factor = {}
        for g in range(gk, groups):
            value = column[g, k] * inverse
            factor[g] = jnp.where(sublane > sk, value, 0.0) if g == gk else value
        for j in range(k + 1, count):
            gj, sj = divmod(j, 8)
            across = spread(column[gj, k][sj : sj + 1])
            for g in range(gj, groups):
                column[g, j] = column[g, j] - factor[g] * across
        pivot_row = spread(part[gk][sk : sk + 1])
        for g in range(gk, groups):
            if g == gk and sk == 7:
                continue
            part[g] = part[g] - jnp.concatenate([factor[g]] * wide, axis=1) * pivot_row
    return jnp.concatenate(
        [part[g] * jnp.concatenate([scale[g]] * wide, axis=1) for g in range(groups)], axis=0
    )


def factor_tile(tile):
    row = lax.broadcasted_iota(jnp.int32, (TILE, TILE), 0)
    lane = lax.broadcasted_iota(jnp.int32, (TILE, TILE), 1)
    both = jnp.concatenate([tile, jnp.where(row == lane, 1.0, 0.0)], axis=1)
    upper = None
    for start in range(0, TILE, GROUP):
        rows = both[start : start + GROUP]
        if upper is not None:
            rows = rows - dot_t(upper[:, start : start + GROUP], upper)
        rows = eliminate(rows, start)
        upper = rows if upper is None else jnp.concatenate([upper, rows], axis=0)
    return upper[:, :TILE], upper[:, TILE:]


def pick_kernel(place, *refs):
    sources, out = refs[:-1], refs[-1]
    for j in range(out.shape[0]):
        for s in range(len(sources)):

            @pl.when(place[j] == s)
            def _():
                out[j] = sources[s][...]


def pick(place, arrays, count):
    shape = arrays[0].shape
    return pl.pallas_call(
        pick_kernel,
        out_shape=jax.ShapeDtypeStruct((count,) + shape, jnp.float32),
        in_specs=[pl.BlockSpec(memory_space=pltpu.SMEM)]
        + [pl.BlockSpec(memory_space=pltpu.VMEM)] * len(arrays),
        out_specs=pl.BlockSpec(memory_space=pltpu.VMEM),
        compiler_params=pltpu.CompilerParams(vmem_limit_bytes=VMEM_LIMIT),
    )(place, *arrays)


def panels_kernel(place, mine, strip, near, far, out, work):
    row_tile, col_tile, core = place[0], place[1], place[2]
    width = work.shape[1]
    right = NB * TILE
    for i in range(NB):
        work[i * TILE : (i + 1) * TILE, right : right + 2 * TILE] = strip[i]

    def place_tiles(source, parity):
        for z in range(ZSRC):
            j = 2 * z + parity
            for t in range(PAYLOAD - 1):
                i = (j + t) % NB
                if t == NB // 2 and j >= NB // 2:
                    continue
                tile = source[z, t * TILE : (t + 1) * TILE, :]
                if i <= j:
                    work[i * TILE : (i + 1) * TILE, j * TILE : (j + 1) * TILE] = tile
                else:
                    work[j * TILE : (j + 1) * TILE, i * TILE : (i + 1) * TILE] = tile.T
            tile = source[z, (PAYLOAD - 1) * TILE :, :]
            work[j * TILE : (j + 1) * TILE, right + 2 * TILE :] = tile.T

    for parity in range(2):

        @pl.when(core == parity)
        def _():
            place_tiles(near, parity)

        @pl.when(core != parity)
        def _():
            place_tiles(far, parity)

    for b in range(NB):
        lo, hi = b * TILE, (b + 1) * TILE
        rows = work[lo:hi, lo:]
        if b:
            rows = rows - dot_t(work[:lo, lo:hi], work[:lo, lo:])
        upper, inverse = factor_tile(rows[:, :TILE])
        work[lo:hi, lo:hi] = upper
        work[lo:hi, hi:] = dot(inverse, rows[:, TILE:])

    mine_row = work[:, right + 2 * TILE :]
    trailing = mine[...] - dot_t(mine_row, work[:, right : right + 2 * TILE])
    out[...] = jnp.where(row_tile >= NB, trailing, 0.0)
    row = lax.broadcasted_iota(jnp.int32, (TILE, TILE), 0)
    lane = lax.broadcasted_iota(jnp.int32, (TILE, TILE), 1)
    for j in range(NB):

        @pl.when(col_tile == j)
        def _():
            tile = work[j * TILE : (j + 1) * TILE, right + 2 * TILE :].T
            keep = row + (row_tile - j) * TILE >= lane
            out[:, :TILE] = jnp.where(keep, tile, 0.0)


def send(array, pairs):
    return lax.ppermute(array, ("row", "col"), pairs)


def device(x, y, z, core):
    return ((x % XS) * YS + y % YS) * (2 * ZS) + (z % ZS) * 2 + core


def per_device(matrix):
    block = matrix.reshape(matrix.shape[1], matrix.shape[2] * matrix.shape[3])
    row_tile = lax.axis_index("row")
    col_tile = lax.axis_index("col")
    x, y = row_tile // YS, row_tile % YS
    z, core = col_tile // 2, col_tile % 2
    columns = [(zz, cc) for zz in range(ZS) for cc in range(2)]
    chips = [(xx, yy) for xx in range(XS) for yy in range(YS)]

    pieces = block
    for step in range(1, XS):
        pairs = [
            (device(0, yy, *col), device(step, yy, *col)) for yy in range(NB) for col in columns
        ]
        arrived = send(block, pairs)
        pieces = jnp.where(x == step, arrived, pieces)
    held = [pieces]
    for step in range(1, YS):
        pairs = [
            (device(xx, yy, *col), device(xx, yy + step, *col))
            for xx in range(XS)
            for yy in range(NB)
            for col in columns
        ]
        held.append(send(pieces, pairs))
    strip = pick((y - jnp.arange(NB, dtype=jnp.int32)) % YS, held, NB)

    first = strip[:, :, :TILE].reshape(NB * TILE, TILE)
    twice = jnp.concatenate([first, first], axis=0)
    start = jnp.minimum(col_tile, NB) * TILE
    payload = jnp.concatenate(
        [
            lax.dynamic_slice_in_dim(twice, start, (PAYLOAD - 1) * TILE, 0),
            block[:, :TILE],
        ],
        axis=0,
    )
    held = [payload]
    for step in range(1, ZS):
        pairs = [
            (device(*chip, zz, cc), device(*chip, zz + step, cc))
            for chip in chips
            for zz in range(ZSRC)
            for cc in range(2)
        ]
        held.append(send(payload, pairs))
    near = pick((z - jnp.arange(ZSRC, dtype=jnp.int32)) % ZS, held, ZSRC)
    pairs = [
        (device(*chip, zz, cc), device(*chip, zz, 1 - cc))
        for chip in chips
        for zz, cc in columns
    ]
    far = send(near, pairs)

    place = jnp.stack([row_tile, col_tile, core]).astype(jnp.int32)
    vmem = pl.BlockSpec(memory_space=pltpu.VMEM)
    result = pl.pallas_call(
        panels_kernel,
        out_shape=jax.ShapeDtypeStruct(block.shape, jnp.float32),
        in_specs=[pl.BlockSpec(memory_space=pltpu.SMEM), vmem, vmem, vmem, vmem],
        out_specs=vmem,
        scratch_shapes=[pltpu.VMEM((NB * TILE, (NB + 3) * TILE), jnp.float32)],
        compiler_params=pltpu.CompilerParams(vmem_limit_bytes=VMEM_LIMIT),
    )(place, block, strip, near, far)
    return result.reshape(matrix.shape)


def solution(mesh):
    placed = (P(None, "row", None, "col"),)
    return jax.shard_map(
        per_device,
        mesh=mesh,
        in_specs=placed,
        out_specs=P(None, "row", None, "col"),
        check_vma=False,
    )
```

time: 1410 us -> 153 us (0.11)
  the two profiles are of different devices: /device:TPU:1 before, /device:TPU:223 now
where the time goes in v1:
time: 153 us
  waiting for transfers between devices  83 us (54%)
  starting transfers between devices  33.2 us (22%)
  Pallas kernels  28.9 us (19%)
  local copies, waits for them, and re-layouts  6.84 us (4%)
    ppermute x18, waiting for transfers between devices, send(): return lax.ppermute(array, ('row', 'col'), pairs)  83 us
    ppermute x18, starting transfers between devices, send(): return lax.ppermute(array, ('row', 'col'), pairs)  33.2 us
    pallas_call x1, Pallas kernels, per_device(): pl.pallas_call(panels_kernel, out_shape=jax.ShapeDtypeStruct(block.shape,...  27.2 us
    unnamed x15, local copies, waits for them, and re-layouts  6.09 us
  transfers between devices with their start and end apart: 18, of which 8 were waited for; matrix products, arithmetic and copies ran while one was open for 0% of the time, Pallas kernels for 0%

profile of v1, /device:TPU:223, one launch (start us, length us, event | category | flops | bytes accessed | tf_op | source)
XLA Modules:
  0.0 152.7 jit_solution(6357724634327960654)
XLA Ops:
  0.0 1.0 copy.6
  2.3 1.3 collective-permute-start
  3.7 7.0 %collective-permute-done = f32[128,256]{1,0:T(8,128)S(1)} collective-permute-done((f32[128,256]{1,0:T(8,128)S(1)}, f32[128,256]{1,0:T(8,128)S(1)}, u32[]{:S(2)}, u32[]{:S(2)}) %collective-permute-start) | collective-permute-done | bytes 131104 | tf_op jit(solution)/shard_map/ppermute | solution.py:159
  10.7 2.1 %collective-permute-start.9 = (f32[128,256]{1,0:T(8,128)S(1)}, f32[128,256]{1,0:T(8,128)S(1)}, u32[]{:S(2)}, u32[]{:S(2)}) collective-permute-start(f32[128,256]{1,0:T(8,128)S(1)} %select_select_fusion.refs_0_), channel_id=1, source_target_pairs={{0,112},{1,113},{2,114},{3,115},{4,116},{5,117},{6,118},{7,119},{8... | collective-permute-start | bytes 393224 | tf_op jit(solution)/shard_map/ppermute | solution.py:159
  12.8 2.0 %collective-permute-start.8 = (f32[128,256]{1,0:T(8,128)S(1)}, f32[128,256]{1,0:T(8,128)S(1)}, u32[]{:S(2)}, u32[]{:S(2)}) collective-permute-start(f32[128,256]{1,0:T(8,128)S(1)} %select_select_fusion.refs_0_), channel_id=1, source_target_pairs={{0,96},{1,97},{2,98},{3,99},{4,100},{5,101},{6,102},{7,103},{8,104... | collective-permute-start | bytes 393224 | tf_op jit(solution)/shard_map/ppermute | solution.py:159
  14.8 1.7 %collective-permute-start.7 = (f32[128,256]{1,0:T(8,128)S(1)}, f32[128,256]{1,0:T(8,128)S(1)}, u32[]{:S(2)}, u32[]{:S(2)}) collective-permute-start(f32[128,256]{1,0:T(8,128)S(1)} %select_select_fusion.refs_0_), channel_id=1, source_target_pairs={{0,80},{1,81},{2,82},{3,83},{4,84},{5,85},{6,86},{7,87},{8,88},{9,... | collective-permute-start | bytes 393224 | tf_op jit(solution)/shard_map/ppermute | solution.py:159
  16.5 1.3 collective-permute-start.6
  17.8 1.9 %collective-permute-start.5 = (f32[128,256]{1,0:T(8,128)S(1)}, f32[128,256]{1,0:T(8,128)S(1)}, u32[]{:S(2)}, u32[]{:S(2)}) collective-permute-start(f32[128,256]{1,0:T(8,128)S(1)} %select_select_fusion.refs_0_), channel_id=1, source_target_pairs={{0,48},{1,49},{2,50},{3,51},{4,52},{5,53},{6,54},{7,55},{8,56},{9,... | collective-permute-start | bytes 393224 | tf_op jit(solution)/shard_map/ppermute | solution.py:159
  19.7 10.8 %collective-permute-start.4 = (f32[128,256]{1,0:T(8,128)S(1)}, f32[128,256]{1,0:T(8,128)S(1)}, u32[]{:S(2)}, u32[]{:S(2)}) collective-permute-start(f32[128,256]{1,0:T(8,128)S(1)} %select_select_fusion.refs_0_), channel_id=1, source_target_pairs={{0,32},{1,33},{2,34},{3,35},{4,36},{5,37},{6,38},{7,39},{8,40},{9,... | collective-permute-start | bytes 393224 | tf_op jit(solution)/shard_map/ppermute | solution.py:159
  30.5 1.9 %collective-permute-start.3 = (f32[128,256]{1,0:T(8,128)S(1)}, f32[128,256]{1,0:T(8,128)S(1)}, u32[]{:S(2)}, u32[]{:S(2)}) collective-permute-start(f32[128,256]{1,0:T(8,128)S(1)} %select_select_fusion.refs_0_), channel_id=1, source_target_pairs={{0,16},{1,17},{2,18},{3,19},{4,20},{5,21},{6,22},{7,23},{8,24},{9,... | collective-permute-start | bytes 393224 | tf_op jit(solution)/shard_map/ppermute | solution.py:159
  32.5 2.4 %collective-permute-done.6.refs_4_ = f32[128,256]{1,0:T(8,128)S(1)} collective-permute-done((f32[128,256]{1,0:T(8,128)S(1)}, f32[128,256]{1,0:T(8,128)S(1)}, u32[]{:S(2)}, u32[]{:S(2)}) %collective-permute-start.6) | collective-permute-done | bytes 131104 | tf_op jit(solution)/shard_map/ppermute | solution.py:159
  34.9 4.6 %collective-permute-done.4.refs_2_ = f32[128,256]{1,0:T(8,128)S(1)} collective-permute-done((f32[128,256]{1,0:T(8,128)S(1)}, f32[128,256]{1,0:T(8,128)S(1)}, u32[]{:S(2)}, u32[]{:S(2)}) %collective-permute-start.4) | collective-permute-done | bytes 131104 | tf_op jit(solution)/shard_map/ppermute | solution.py:159
  39.6 4.9 %collective-permute-done.3.refs_1_ = f32[128,256]{1,0:T(8,128)S(1)} collective-permute-done((f32[128,256]{1,0:T(8,128)S(1)}, f32[128,256]{1,0:T(8,128)S(1)}, u32[]{:S(2)}, u32[]{:S(2)}) %collective-permute-start.3) | collective-permute-done | bytes 131104 | tf_op jit(solution)/shard_map/ppermute | solution.py:159
  44.5 0.9 shard_map.17.strip
  45.6 0.7 collective-permute-start.16
  48.4 1.3 collective-permute-start.12
  49.7 1.3 collective-permute-start.11
  51.0 1.3 collective-permute-start.10
  52.4 19.8 %collective-permute-done.12.refs_3_ = f32[640,128]{1,0:T(8,128)S(1)} collective-permute-done((f32[640,128]{1,0:T(8,128)S(1)}, f32[640,128]{1,0:T(8,128)S(1)}, u32[]{:S(2)}, u32[]{:S(2)}) %collective-permute-start.12) | collective-permute-done | bytes 327712 | tf_op jit(solution)/shard_map/ppermute | solution.py:159
  72.2 0.7 copy-done
  72.9 21.9 %collective-permute-done.11.refs_2_ = f32[640,128]{1,0:T(8,128)S(1)} collective-permute-done((f32[640,128]{1,0:T(8,128)S(1)}, f32[640,128]{1,0:T(8,128)S(1)}, u32[]{:S(2)}, u32[]{:S(2)}) %collective-permute-start.11) | collective-permute-done | bytes 327712 | tf_op jit(solution)/shard_map/ppermute | solution.py:159
  94.7 0.7 copy-done.2
  95.5 20.3 %collective-permute-done.10.refs_1_ = f32[640,128]{1,0:T(8,128)S(1)} collective-permute-done((f32[640,128]{1,0:T(8,128)S(1)}, f32[640,128]{1,0:T(8,128)S(1)}, u32[]{:S(2)}, u32[]{:S(2)}) %collective-permute-start.10) | collective-permute-done | bytes 327712 | tf_op jit(solution)/shard_map/ppermute | solution.py:159
  115.7 0.7 copy-done.4
  116.5 1.0 copy-done.1
  117.4 1.0 copy-done.3
  118.4 1.0 copy-done.5
  119.4 0.8 shard_map.18.near
  120.2 2.4 %collective-permute-start.17 = (f32[3,640,128]{2,1,0:T(8,128)S(1)}, f32[3,640,128]{2,1,0:T(8,128)S(1)}, u32[]{:S(2)}, u32[]{:S(2)}) collective-permute-start(f32[3,640,128]{2,1,0:T(8,128)S(1)} %shard_map.18.near), channel_id=1, source_target_pairs={{0,1},{1,0},{2,3},{3,2},{4,5},{5,4},{6,7},{7,6},{8,9},{9,8},{10,11... | collective-permute-start | bytes 2949128 | tf_op jit(solution)/shard_map/ppermute | solution.py:159
  122.7 2.1 %collective-permute-done.17.far = f32[3,640,128]{2,1,0:T(8,128)S(1)} collective-permute-done((f32[3,640,128]{2,1,0:T(8,128)S(1)}, f32[3,640,128]{2,1,0:T(8,128)S(1)}, u32[]{:S(2)}, u32[]{:S(2)}) %collective-permute-start.17) | collective-permute-done | bytes 983072 | tf_op jit(solution)/shard_map/ppermute | solution.py:159
  124.7 27.2 %shard_map.19 = f32[128,256]{1,0:T(8,128)S(1)} custom-call(s32[3]{0:T(128)S(1)} %pad_add_fusion.place, f32[128,256]{1,0:T(8,128)S(1)} %bitcast.15, f32[6,128,256]{2,1,0:T(8,128)S(1)} %shard_map.17.strip, f32[3,640,128]{2,1,0:T(8,128)S(1)} %shard_map.18.near, f32[3,640,128]{2,1,0:T(8,128)S(1)} %collective-permute-done.17.far), custom_call_target="tpu_custom_call" | custom-call | tf_op jit(solution)/shard_map/pallas_call | solution.py:222
  152.0 0.7 reshape.11
  (31 shorter events, 3.8 us)
Async XLA Ops:
  0.0 10.7 %copy-start.6 = (f32[1,128,2,128]{3,2,1,0:T(2,128)S(1)}, f32[1,128,2,128]{3,2,1,0:T(2,128)}, u32[]{:S(2)}) copy-start(f32[1,128,2,128]{3,2,1,0:T(2,128)} %param.1) | copy-start | bytes 393220
  1.0 2.7 %collective-permute-start.2 = (f32[128,256]{1,0:T(8,128)S(1)}, f32[128,256]{1,0:T(8,128)S(1)}, u32[]{:S(2)}, u32[]{:S(2)}) collective-permute-start(f32[128,256]{1,0:T(8,128)S(1)} %bitcast.11), channel_id=1, source_target_pairs={{0,128},{1,129},{2,130},{3,131},{4,132},{5,133},{6,134},{7,135},{8... | collective-permute-start | bytes 393224 | tf_op jit(solution)/shard_map/ppermute | solution.py:159
  1.7 2.0 %collective-permute-start.1 = (f32[128,256]{1,0:T(8,128)S(1)}, f32[128,256]{1,0:T(8,128)S(1)}, u32[]{:S(2)}, u32[]{:S(2)}) collective-permute-start(f32[128,256]{1,0:T(8,128)S(1)} %bitcast.12), channel_id=1, source_target_pairs={{0,256},{1,257},{2,258},{3,259},{4,260},{5,261},{6,262},{7,263},{8... | collective-permute-start | bytes 393224 | tf_op jit(solution)/shard_map/ppermute | solution.py:159
  2.3 8.4 %collective-permute-start = (f32[128,256]{1,0:T(8,128)S(1)}, f32[128,256]{1,0:T(8,128)S(1)}, u32[]{:S(2)}, u32[]{:S(2)}) collective-permute-start(f32[128,256]{1,0:T(8,128)S(1)} %bitcast.13), channel_id=1, source_target_pairs={{0,384},{1,385},{2,386},{3,387},{4,388},{5,389},{6,390},{7,391},{8... | collective-permute-start | bytes 393224 | tf_op jit(solution)/shard_map/ppermute | solution.py:159
  10.7 9.0 %collective-permute-start.9 = (f32[128,256]{1,0:T(8,128)S(1)}, f32[128,256]{1,0:T(8,128)S(1)}, u32[]{:S(2)}, u32[]{:S(2)}) collective-permute-start(f32[128,256]{1,0:T(8,128)S(1)} %select_select_fusion.refs_0_), channel_id=1, source_target_pairs={{0,112},{1,113},{2,114},{3,115},{4,116},{5,117},{6,118},{7,119},{8... | collective-permute-start | bytes 393224 | tf_op jit(solution)/shard_map/ppermute | solution.py:159
  12.8 17.7 %collective-permute-start.8 = (f32[128,256]{1,0:T(8,128)S(1)}, f32[128,256]{1,0:T(8,128)S(1)}, u32[]{:S(2)}, u32[]{:S(2)}) collective-permute-start(f32[128,256]{1,0:T(8,128)S(1)} %select_select_fusion.refs_0_), channel_id=1, source_target_pairs={{0,96},{1,97},{2,98},{3,99},{4,100},{5,101},{6,102},{7,103},{8,104... | collective-permute-start | bytes 393224 | tf_op jit(solution)/shard_map/ppermute | solution.py:159
  14.8 17.7 %collective-permute-start.7 = (f32[128,256]{1,0:T(8,128)S(1)}, f32[128,256]{1,0:T(8,128)S(1)}, u32[]{:S(2)}, u32[]{:S(2)}) collective-permute-start(f32[128,256]{1,0:T(8,128)S(1)} %select_select_fusion.refs_0_), channel_id=1, source_target_pairs={{0,80},{1,81},{2,82},{3,83},{4,84},{5,85},{6,86},{7,87},{8,88},{9,... | collective-permute-start | bytes 393224 | tf_op jit(solution)/shard_map/ppermute | solution.py:159
  16.5 18.4 %collective-permute-start.6 = (f32[128,256]{1,0:T(8,128)S(1)}, f32[128,256]{1,0:T(8,128)S(1)}, u32[]{:S(2)}, u32[]{:S(2)}) collective-permute-start(f32[128,256]{1,0:T(8,128)S(1)} %select_select_fusion.refs_0_), channel_id=1, source_target_pairs={{0,64},{1,65},{2,66},{3,67},{4,68},{5,69},{6,70},{7,71},{8,72},{9,... | collective-permute-start | bytes 393224 | tf_op jit(solution)/shard_map/ppermute | solution.py:159
  17.8 17.1 %collective-permute-start.5 = (f32[128,256]{1,0:T(8,128)S(1)}, f32[128,256]{1,0:T(8,128)S(1)}, u32[]{:S(2)}, u32[]{:S(2)}) collective-permute-start(f32[128,256]{1,0:T(8,128)S(1)} %select_select_fusion.refs_0_), channel_id=1, source_target_pairs={{0,48},{1,49},{2,50},{3,51},{4,52},{5,53},{6,54},{7,55},{8,56},{9,... | collective-permute-start | bytes 393224 | tf_op jit(solution)/shard_map/ppermute | solution.py:159
  19.7 19.8 %collective-permute-start.4 = (f32[128,256]{1,0:T(8,128)S(1)}, f32[128,256]{1,0:T(8,128)S(1)}, u32[]{:S(2)}, u32[]{:S(2)}) collective-permute-start(f32[128,256]{1,0:T(8,128)S(1)} %select_select_fusion.refs_0_), channel_id=1, source_target_pairs={{0,32},{1,33},{2,34},{3,35},{4,36},{5,37},{6,38},{7,39},{8,40},{9,... | collective-permute-start | bytes 393224 | tf_op jit(solution)/shard_map/ppermute | solution.py:159
  30.5 14.0 %collective-permute-start.3 = (f32[128,256]{1,0:T(8,128)S(1)}, f32[128,256]{1,0:T(8,128)S(1)}, u32[]{:S(2)}, u32[]{:S(2)}) collective-permute-start(f32[128,256]{1,0:T(8,128)S(1)} %select_select_fusion.refs_0_), channel_id=1, source_target_pairs={{0,16},{1,17},{2,18},{3,19},{4,20},{5,21},{6,22},{7,23},{8,24},{9,... | collective-permute-start | bytes 393224 | tf_op jit(solution)/shard_map/ppermute | solution.py:159
  45.6 4.1 %collective-permute-start.16 = (f32[640,128]{1,0:T(8,128)S(1)}, f32[640,128]{1,0:T(8,128)S(1)}, u32[]{:S(2)}, u32[]{:S(2)}) collective-permute-start(f32[640,128]{1,0:T(8,128)S(1)} %pad_maximum_fusion.refs_0_), channel_id=1, source_target_pairs={{0,14},{1,15},{2,0},{3,1},{4,2},{5,3},{16,30},{17,31},{18,16},{19,... | collective-permute-start | bytes 983048 | tf_op jit(solution)/shard_map/ppermute | solution.py:159
  46.3 4.7 %collective-permute-start.15 = (f32[640,128]{1,0:T(8,128)S(1)}, f32[640,128]{1,0:T(8,128)S(1)}, u32[]{:S(2)}, u32[]{:S(2)}) collective-permute-start(f32[640,128]{1,0:T(8,128)S(1)} %pad_maximum_fusion.refs_0_), channel_id=1, source_target_pairs={{0,12},{1,13},{2,14},{3,15},{4,0},{5,1},{16,28},{17,29},{18,30},{1... | collective-permute-start | bytes 983048 | tf_op jit(solution)/shard_map/ppermute | solution.py:159
  47.0 5.3 %collective-permute-start.14 = (f32[640,128]{1,0:T(8,128)S(1)}, f32[640,128]{1,0:T(8,128)S(1)}, u32[]{:S(2)}, u32[]{:S(2)}) collective-permute-start(f32[640,128]{1,0:T(8,128)S(1)} %pad_maximum_fusion.refs_0_), channel_id=1, source_target_pairs={{0,10},{1,11},{2,12},{3,13},{4,14},{5,15},{16,26},{17,27},{18,28},... | collective-permute-start | bytes 983048 | tf_op jit(solution)/shard_map/ppermute | solution.py:159
  47.7 4.7 %collective-permute-start.13 = (f32[640,128]{1,0:T(8,128)S(1)}, f32[640,128]{1,0:T(8,128)S(1)}, u32[]{:S(2)}, u32[]{:S(2)}) collective-permute-start(f32[640,128]{1,0:T(8,128)S(1)} %pad_maximum_fusion.refs_0_), channel_id=1, source_target_pairs={{0,8},{1,9},{2,10},{3,11},{4,12},{5,13},{16,24},{17,25},{18,26},{1... | collective-permute-start | bytes 983048 | tf_op jit(solution)/shard_map/ppermute | solution.py:159
  48.4 23.8 %collective-permute-start.12 = (f32[640,128]{1,0:T(8,128)S(1)}, f32[640,128]{1,0:T(8,128)S(1)}, u32[]{:S(2)}, u32[]{:S(2)}) collective-permute-start(f32[640,128]{1,0:T(8,128)S(1)} %pad_maximum_fusion.refs_0_), channel_id=1, source_target_pairs={{0,6},{1,7},{2,8},{3,9},{4,10},{5,11},{16,22},{17,23},{18,24},{19,... | collective-permute-start | bytes 983048 | tf_op jit(solution)/shard_map/ppermute | solution.py:159
  49.7 45.0 %collective-permute-start.11 = (f32[640,128]{1,0:T(8,128)S(1)}, f32[640,128]{1,0:T(8,128)S(1)}, u32[]{:S(2)}, u32[]{:S(2)}) collective-permute-start(f32[640,128]{1,0:T(8,128)S(1)} %pad_maximum_fusion.refs_0_), channel_id=1, source_target_pairs={{0,4},{1,5},{2,6},{3,7},{4,8},{5,9},{16,20},{17,21},{18,22},{19,23... | collective-permute-start | bytes 983048 | tf_op jit(solution)/shard_map/ppermute | solution.py:159
  51.0 64.7 %collective-permute-start.10 = (f32[640,128]{1,0:T(8,128)S(1)}, f32[640,128]{1,0:T(8,128)S(1)}, u32[]{:S(2)}, u32[]{:S(2)}) collective-permute-start(f32[640,128]{1,0:T(8,128)S(1)} %pad_maximum_fusion.refs_0_), channel_id=1, source_target_pairs={{0,2},{1,3},{2,4},{3,5},{4,6},{5,7},{16,18},{17,19},{18,20},{19,21... | collective-permute-start | bytes 983048 | tf_op jit(solution)/shard_map/ppermute | solution.py:159
  72.2 0.7 copy-start
  94.7 0.7 copy-start.2
  115.7 0.7 copy-start.4
  116.5 1.0 copy-start.1
  117.4 1.0 copy-start.3
  118.4 1.0 copy-start.5
  120.2 4.6 %collective-permute-start.17 = (f32[3,640,128]{2,1,0:T(8,128)S(1)}, f32[3,640,128]{2,1,0:T(8,128)S(1)}, u32[]{:S(2)}, u32[]{:S(2)}) collective-permute-start(f32[3,640,128]{2,1,0:T(8,128)S(1)} %shard_map.18.near), channel_id=1, source_target_pairs={{0,1},{1,0},{2,3},{3,2},{4,5},{5,4},{6,7},{7,6},{8,9},{9,8},{10,11... | collective-permute-start | bytes 2949128 | tf_op jit(solution)/shard_map/ppermute | solution.py:159

commit v2 on v1

v2 whole, which is shorter than its diff:
```python
import jax
import jax.numpy as jnp
from jax import lax
from jax.experimental import pallas as pl
from jax.experimental.pallas import tpu as pltpu
from jax.sharding import PartitionSpec as P

TILE = 128
NB = 6
GROUP = 32
XS, YS, ZS = 4, 8, 8
ZSRC = NB // 2
VMEM_LIMIT = 48 * 1024 * 1024
HI = lax.Precision.HIGHEST


def dot(a, b):
    return lax.dot_general(a, b, (((1,), (0,)), ((), ())), precision=HI, preferred_element_type=jnp.float32)


def dot_t(a, b):
    return lax.dot_general(a, b, (((0,), (0,)), ((), ())), precision=HI, preferred_element_type=jnp.float32)


def spread(row):
    return jnp.broadcast_to(row, (8, row.shape[1]))


def eliminate(rows, offset):
    count, width = rows.shape
    groups = count // 8
    wide = width // TILE
    block = rows[:, offset : offset + count]
    column = {}
    for j in range(count):
        for g in range(j // 8, groups):
            column[g, j] = jnp.broadcast_to(block[8 * g : 8 * g + 8, j : j + 1], (8, TILE))
    part = [rows[8 * g : 8 * g + 8] for g in range(groups)]
    sublane = lax.broadcasted_iota(jnp.int32, (8, TILE), 0)
    scale = [None] * groups
    for k in range(count):
        gk, sk = divmod(k, 8)
        pivot = spread(column[gk, k][sk : sk + 1])
        inverse = pl.reciprocal(pivot)
        root = lax.rsqrt(pivot)
        scale[gk] = root if scale[gk] is None else jnp.where(sublane == sk, root, scale[gk])
        factor = {}
        for g in range(gk, groups):
            value = column[g, k] * inverse
            factor[g] = jnp.where(sublane > sk, value, 0.0) if g == gk else value
        for j in range(k + 1, count):
            gj, sj = divmod(j, 8)
            across = spread(column[gj, k][sj : sj + 1])
            for g in range(gj, groups):
                column[g, j] = column[g, j] - factor[g] * across
        pivot_row = spread(part[gk][sk : sk + 1])
        for g in range(gk, groups):
            if g == gk and sk == 7:
                continue
            part[g] = part[g] - jnp.concatenate([factor[g]] * wide, axis=1) * pivot_row
    return jnp.concatenate(
        [part[g] * jnp.concatenate([scale[g]] * wide, axis=1) for g in range(groups)], axis=0
    )


def factor_tile(tile):
    row = lax.broadcasted_iota(jnp.int32, (TILE, TILE), 0)
    lane = lax.broadcasted_iota(jnp.int32, (TILE, TILE), 1)
    both = jnp.concatenate([tile, jnp.where(row == lane, 1.0, 0.0)], axis=1)
    upper = None
    for start in range(0, TILE, GROUP):
        rows = both[start : start + GROUP]
        if upper is not None:
            rows = rows - dot_t(upper[:, start : start + GROUP], upper)
        rows = eliminate(rows, start)
        upper = rows if upper is None else jnp.concatenate([upper, rows], axis=0)
    return upper[:, :TILE], upper[:, TILE:]


def dot_nt(a, b):
    return lax.dot_general(a, b, (((1,), (1,)), ((), ())), precision=HI, preferred_element_type=jnp.float32)


def factor_kernel(place, near, far, inverse, upper):
    core = place[2]

    def place_tiles(source, shift):
        for i in range(NB):
            if (i + shift) % 2 != place_tiles.parity:
                continue
            for half in range(2):
                distance = shift + 2 * half
                j = (i + distance) % NB
                if distance == NB // 2 and i >= NB // 2:
                    continue
                tile = source[i, half * TILE : (half + 1) * TILE, :]
                if i <= j:
                    upper[i * TILE : (i + 1) * TILE, j * TILE : (j + 1) * TILE] = tile
                else:
                    upper[j * TILE : (j + 1) * TILE, i * TILE : (i + 1) * TILE] = tile.T

    for parity in range(2):

        @pl.when(core == parity)
        def _():
            for source, held in ((near, parity), (far, 1 - parity)):
                place_tiles.parity = held
                place_tiles(source, 0)
                place_tiles(source, 1)

    for b in range(NB):
        lo, hi = b * TILE, (b + 1) * TILE
        rows = upper[lo:hi, lo:]
        if b:
            rows = rows - dot_t(upper[:lo, lo:hi], upper[:lo, lo:])
        _, own = factor_tile(rows[:, :TILE])
        inverse[lo:hi, lo:hi] = own
        if hi < NB * TILE:
            upper[lo:hi, hi:] = dot(own, rows[:, TILE:])
            inverse[lo:hi, hi:] = jnp.zeros((TILE, NB * TILE - hi), jnp.float32)
        if b:
            inverse[lo:hi, :lo] = -dot(own, dot_t(upper[:lo, lo:hi], inverse[:lo, :lo]))


def update_kernel(place, mine, strip, near, far, inverse, out, row_strip, solved):
    row_tile, col_tile, core = place[0], place[1], place[2]

    for parity in range(2):

        @pl.when(core == parity)
        def _():
            for j in range(NB):
                source = near if j % 2 == parity else far
                row_strip[:, j * TILE : (j + 1) * TILE] = source[j // 2]

    panel = []
    for b in range(NB):
        hi = (b + 1) * TILE
        lower = inverse[b * TILE : hi, :hi]
        total = None
        for i in range(b + 1):
            term = dot(lower[:, i * TILE : (i + 1) * TILE], strip[i])
            total = term if total is None else total + term
        solved[b * TILE : hi, :] = total
        panel.append(dot_nt(row_strip[:, :hi], lower))
    trailing = mine[...] - dot(jnp.concatenate(panel, axis=1), solved[...])
    out[...] = jnp.where(row_tile >= NB, trailing, 0.0)
    row = lax.broadcasted_iota(jnp.int32, (TILE, TILE), 0)
    lane = lax.broadcasted_iota(jnp.int32, (TILE, TILE), 1)
    for j in range(NB):

        @pl.when(col_tile == j)
        def _():
            keep = row + (row_tile - j) * TILE >= lane
            out[:, :TILE] = jnp.where(keep, panel[j], 0.0)


def send(array, pairs):
    return lax.ppermute(array, ("row", "col"), pairs)


def device(x, y, z, core):
    return ((x % XS) * YS + y % YS) * (2 * ZS) + (z % ZS) * 2 + core


CHIPS = [(x, y) for x in range(XS) for y in range(YS)]
COLUMNS = [(z, core) for z in range(ZS) for core in range(2)]
Y_GROUPS = [[x * YS + y for y in range(YS)] for x in range(XS)]
Z_GROUPS = [[z * 2 + core for z in range(ZS)] for core in range(2)]


def along_x(array, x):
    result = array
    for step in range(1, XS):
        pairs = [(device(0, y, *col), device(step, y, *col)) for y in range(NB) for col in COLUMNS]
        result = jnp.where(x == step, send(array, pairs), result)
    return result


def to_all(array, axis, groups):
    copies = jnp.broadcast_to(array, (len(groups[0]),) + array.shape)
    return lax.all_to_all(copies, axis, 0, 0, axis_index_groups=groups)


def per_device(matrix):
    block = matrix.reshape(matrix.shape[1], matrix.shape[2] * matrix.shape[3])
    row_tile = lax.axis_index("row")
    col_tile = lax.axis_index("col")
    x = row_tile // YS
    core = col_tile % 2

    strip = lax.all_gather(along_x(block, x), "row", axis_index_groups=Y_GROUPS)

    near_row = to_all(block[:, :TILE], "col", Z_GROUPS)[:ZSRC]

    first = jnp.where(row_tile % 2 == core, row_tile, (row_tile + 1) % NB)
    start = jnp.clip((first - core) // 2, 0, ZSRC - 1)
    wrapped = jnp.concatenate([near_row, near_row[:1]], axis=0)
    tiles = lax.dynamic_slice_in_dim(wrapped, start, 2, 0).reshape(2 * TILE, TILE)
    near = to_all(along_x(tiles, x), "row", Y_GROUPS)[:NB]

    swap = [(device(*chip, z, c), device(*chip, z, 1 - c)) for chip in CHIPS for z, c in COLUMNS]
    far = send(near, swap)
    far_row = send(near_row, swap)

    place = jnp.stack([row_tile, col_tile, core]).astype(jnp.int32)
    smem = pl.BlockSpec(memory_space=pltpu.SMEM)
    vmem = pl.BlockSpec(memory_space=pltpu.VMEM)
    params = pltpu.CompilerParams(vmem_limit_bytes=VMEM_LIMIT)
    order = NB * TILE
    inverse = pl.pallas_call(
        factor_kernel,
        out_shape=jax.ShapeDtypeStruct((order, order), jnp.float32),
        in_specs=[smem, vmem, vmem],
        out_specs=vmem,
        scratch_shapes=[pltpu.VMEM((order, order), jnp.float32)],
        compiler_params=params,
        cost_estimate=pl.CostEstimate(flops=4 * 10**9, bytes_accessed=8 * 10**6, transcendentals=0),
    )(place, near, far)
    result = pl.pallas_call(
        update_kernel,
        out_shape=jax.ShapeDtypeStruct(block.shape, jnp.float32),
        in_specs=[smem, vmem, vmem, vmem, vmem, vmem],
        out_specs=vmem,
        scratch_shapes=[pltpu.VMEM((TILE, order), jnp.float32), pltpu.VMEM((order, 2 * TILE), jnp.float32)],
        compiler_params=params,
    )(place, block, strip, near_row, far_row, inverse)
    return result.reshape(matrix.shape)


def solution(mesh):
    placed = (P(None, "row", None, "col"),)
    return jax.shard_map(
        per_device,
        mesh=mesh,
        in_specs=placed,
        out_specs=P(None, "row", None, "col"),
        check_vma=False,
    )
```

time: 153 us -> 132 us (0.86)
  the two profiles are of different devices: /device:TPU:223 before, /device:TPU:1 now
where the time goes in v2:
time: 132 us; the launch traced here: 130 us
  waiting for transfers between devices  43.6 us (33%)
  starting transfers between devices  35 us (27%)
  Pallas kernels  32.2 us (24%)
  between operations  13.6 us (10%)
  local copies, waits for them, and re-layouts  4.82 us (4%)
    all_to_all x2, waiting for transfers between devices, to_all(): return lax.all_to_all(copies, axis, 0, 0, axis_index_groups=groups)  37.5 us
    pallas_call x1, Pallas kernels, per_device(): pl.pallas_call(factor_kernel, out_shape=jax.ShapeDtypeStruct((order, orde...  27.1 us
    all_to_all x2, starting transfers between devices, to_all(): return lax.all_to_all(copies, axis, 0, 0, axis_index_groups=groups)  17.7 us
    ppermute x8, starting transfers between devices, send(): return lax.ppermute(array, ('row', 'col'), pairs)  17.2 us
    ppermute x8, waiting for transfers between devices, send(): return lax.ppermute(array, ('row', 'col'), pairs)  6.06 us
    pallas_call x1, Pallas kernels, per_device(): pl.pallas_call(update_kernel, out_shape=jax.ShapeDtypeStruct(block.shape,...  5.1 us
  transfers between devices with their start and end apart: 11, of which 5 were waited for; matrix products, arithmetic and copies ran while one was open for 1% of the time, Pallas kernels for 21%

profile of v2, /device:TPU:1, one launch (start us, length us, event | category | flops | bytes accessed | tf_op | source)
XLA Modules:
  0.0 130.0 jit_solution(13273356097196557425)
XLA Ops:
  6.5 0.9 copy.6
  7.5 0.8 broadcast_in_dim.6
  8.3 10.9 %all-to-all-start = ((f32[8,128,128]{2,1,0:T(8,128)}), f32[8,128,128]{2,1,0:T(8,128)S(1)}, u32[]{:S(2)}, u32[]{:S(2)}) async-start(f32[8,128,128]{2,1,0:T(8,128)} %broadcast_in_dim.6), calls=%async_computation | async-start | bytes 1048576 | tf_op jit(solution)/shard_map/all_to_all | solution.py:182
  19.2 18.0 %all-to-all-done = f32[8,128,128]{2,1,0:T(8,128)S(1)} async-done(((f32[8,128,128]{2,1,0:T(8,128)}), f32[8,128,128]{2,1,0:T(8,128)S(1)}, u32[]{:S(2)}, u32[]{:S(2)}) %all-to-all-start) | async-done | bytes 524320 | tf_op jit(solution)/shard_map/all_to_all | solution.py:182
  37.2 4.4 %collective-permute-start.4 = (f32[256,128]{1,0:T(8,128)S(1)}, f32[256,128]{1,0:T(8,128)S(1)}, u32[]{:S(2)}, u32[]{:S(2)}) collective-permute-start(f32[256,128]{1,0:T(8,128)S(1)} %bitcast.21), channel_id=1, source_target_pairs={{0,384},{1,385},{2,386},{3,387},{4,388},{5,389},{6,390},{7,391},{8... | collective-permute-start | bytes 393224 | tf_op jit(solution)/shard_map/ppermute | solution.py:159
  41.6 1.3 collective-permute-start.5
  42.9 1.3 collective-permute-start.6
  44.2 0.0 collective-permute-done.4
  44.2 1.0 collective-permute-done.5
  45.2 2.8 %collective-permute-done.6 = f32[256,128]{1,0:T(8,128)S(1)} collective-permute-done((f32[256,128]{1,0:T(8,128)S(1)}, f32[256,128]{1,0:T(8,128)S(1)}, u32[]{:S(2)}, u32[]{:S(2)}) %collective-permute-start.6) | collective-permute-done | bytes 131104 | tf_op jit(solution)/shard_map/ppermute | solution.py:159
  48.1 1.1 broadcast_in_dim.7
  49.1 6.8 %all-to-all-start.1 = ((f32[8,256,128]{2,1,0:T(8,128)}), f32[8,256,128]{2,1,0:T(8,128)S(1)}, u32[]{:S(2)}, u32[]{:S(2)}) async-start(f32[8,256,128]{2,1,0:T(8,128)} %broadcast_in_dim.7), calls=%async_computation.1 | async-start | bytes 2097152 | tf_op jit(solution)/shard_map/all_to_all | solution.py:182
  56.0 0.0 all-gather.3.cloned.1.call-start
  56.0 1.3 collective-permute-start
  57.3 2.2 %collective-permute-start.1 = (f32[128,256]{1,0:T(8,128)S(1)}, f32[128,256]{1,0:T(8,128)S(1)}, u32[]{:S(2)}, u32[]{:S(2)}) collective-permute-start(f32[128,256]{1,0:T(8,128)S(1)} %bitcast.16), channel_id=1, source_target_pairs={{0,256},{1,257},{2,258},{3,259},{4,260},{5,261},{6,262},{7,263},{8... | collective-permute-start | bytes 393224 | tf_op jit(solution)/shard_map/ppermute | solution.py:159
  59.5 2.0 %collective-permute-start.2 = (f32[128,256]{1,0:T(8,128)S(1)}, f32[128,256]{1,0:T(8,128)S(1)}, u32[]{:S(2)}, u32[]{:S(2)}) collective-permute-start(f32[128,256]{1,0:T(8,128)S(1)} %bitcast.17), channel_id=1, source_target_pairs={{0,128},{1,129},{2,130},{3,131},{4,132},{5,133},{6,134},{7,135},{8... | collective-permute-start | bytes 393224 | tf_op jit(solution)/shard_map/ppermute | solution.py:159
  61.5 0.0 collective-permute-done
  61.5 2.2 %collective-permute-done.2 = f32[128,256]{1,0:T(8,128)S(1)} collective-permute-done((f32[128,256]{1,0:T(8,128)S(1)}, f32[128,256]{1,0:T(8,128)S(1)}, u32[]{:S(2)}, u32[]{:S(2)}) %collective-permute-start.2) | collective-permute-done | bytes 131104 | tf_op jit(solution)/shard_map/ppermute | solution.py:159
  63.7 0.7 select_select_fusion.1
  64.4 0.0 all-gather.3.cloned.1.call-update
  64.4 19.5 %all-to-all-done.1 = f32[8,256,128]{2,1,0:T(8,128)S(1)} async-done(((f32[8,256,128]{2,1,0:T(8,128)}), f32[8,256,128]{2,1,0:T(8,128)S(1)}, u32[]{:S(2)}, u32[]{:S(2)}) %all-to-all-start.1) | async-done | bytes 1048608 | tf_op jit(solution)/shard_map/all_to_all | solution.py:182
  84.0 0.1 slice.20.near
  84.0 2.9 %collective-permute-start.7 = (f32[6,256,128]{2,1,0:T(8,128)S(1)}, f32[6,256,128]{2,1,0:T(8,128)S(1)}, u32[]{:S(2)}, u32[]{:S(2)}) collective-permute-start(f32[6,256,128]{2,1,0:T(8,128)S(1)} %slice.20.near), channel_id=1, source_target_pairs={{0,1},{1,0},{2,3},{3,2},{4,5},{5,4},{6,7},{7,6},{8,9},{9,8},{10,11... | collective-permute-start | bytes 2359304 | tf_op jit(solution)/shard_map/ppermute | solution.py:159
  86.9 0.1 pad_add_fusion.place
  87.0 1.9 %collective-permute-start.3 = (f32[3,128,128]{2,1,0:T(8,128)S(1)}, f32[3,128,128]{2,1,0:T(8,128)S(1)}, u32[]{:S(2)}, u32[]{:S(2)}) collective-permute-start(f32[3,128,128]{2,1,0:T(8,128)S(1)} %slice.18.near), channel_id=1, source_target_pairs={{0,1},{1,0},{2,3},{3,2},{4,5},{5,4},{6,7},{7,6},{8,9},{9,8},{10,11... | collective-permute-start | bytes 589832 | tf_op jit(solution)/shard_map/ppermute | solution.py:159
  88.9 0.0 collective-permute-done.7.far
  88.9 27.1 %shard_map.17.inverse = f32[768,768]{1,0:T(8,128)S(1)} custom-call(s32[3]{0:T(128)S(1)} %pad_add_fusion.place, f32[6,256,128]{2,1,0:T(8,128)S(1)} %slice.20.near, f32[6,256,128]{2,1,0:T(8,128)S(1)} %collective-permute-done.7.far), custom_call_target="tpu_custom_call" | custom-call | flops 4000000000 | bytes 8000000 | tf_op jit(solution)/shard_map/pallas_call | solution.py:211
  116.1 0.0 collective-permute-done.3.far
  116.1 0.0 all-gather.3.cloned.1.call-done
  116.1 1.2 copy-done
  117.3 5.1 %shard_map.18 = f32[128,256]{1,0:T(8,128)S(1)} custom-call(s32[3]{0:T(128)S(1)} %pad_add_fusion.place, f32[128,256]{1,0:T(8,128)S(1)} %bitcast.18, f32[8,128,256]{2,1,0:T(8,128)S(1)} %bitcast.13, f32[3,128,128]{2,1,0:T(8,128)S(1)} %slice.18.near, f32[3,128,128]{2,1,0:T(8,128)S(1)} %collective-permute-done.3.far, f32[768,768]{1,0:T(8,128)S(1)} %shard_map.17.inverse), custom_call_target="tpu_custom_call" | custom-call | tf_op jit(solution)/shard_map/pallas_call | solution.py:220
  122.4 0.7 reshape.11
  (9 shorter events, 0.1 us)
Async XLA Ops:
  8.3 28.8 %all-to-all-start = ((f32[8,128,128]{2,1,0:T(8,128)}), f32[8,128,128]{2,1,0:T(8,128)S(1)}, u32[]{:S(2)}, u32[]{:S(2)}) async-start(f32[8,128,128]{2,1,0:T(8,128)} %broadcast_in_dim.6), calls=%async_computation | async-start | bytes 1048576 | tf_op jit(solution)/shard_map/all_to_all | solution.py:182
  19.2 44.6 %copy-start.1 = (f32[1,128,2,128]{3,2,1,0:T(2,128)S(1)}, f32[1,128,2,128]{3,2,1,0:T(2,128)}, u32[]{:S(2)}) copy-start(f32[1,128,2,128]{3,2,1,0:T(2,128)} %param.1) | copy-start | bytes 393220
  37.2 7.0 %collective-permute-start.4 = (f32[256,128]{1,0:T(8,128)S(1)}, f32[256,128]{1,0:T(8,128)S(1)}, u32[]{:S(2)}, u32[]{:S(2)}) collective-permute-start(f32[256,128]{1,0:T(8,128)S(1)} %bitcast.21), channel_id=1, source_target_pairs={{0,384},{1,385},{2,386},{3,387},{4,388},{5,389},{6,390},{7,391},{8... | collective-permute-start | bytes 393224 | tf_op jit(solution)/shard_map/ppermute | solution.py:159
  41.6 3.7 %collective-permute-start.5 = (f32[256,128]{1,0:T(8,128)S(1)}, f32[256,128]{1,0:T(8,128)S(1)}, u32[]{:S(2)}, u32[]{:S(2)}) collective-permute-start(f32[256,128]{1,0:T(8,128)S(1)} %bitcast.22), channel_id=1, source_target_pairs={{0,256},{1,257},{2,258},{3,259},{4,260},{5,261},{6,262},{7,263},{8... | collective-permute-start | bytes 393224 | tf_op jit(solution)/shard_map/ppermute | solution.py:159
  42.9 5.2 %collective-permute-start.6 = (f32[256,128]{1,0:T(8,128)S(1)}, f32[256,128]{1,0:T(8,128)S(1)}, u32[]{:S(2)}, u32[]{:S(2)}) collective-permute-start(f32[256,128]{1,0:T(8,128)S(1)} %bitcast.23), channel_id=1, source_target_pairs={{0,128},{1,129},{2,130},{3,131},{4,132},{5,133},{6,134},{7,135},{8... | collective-permute-start | bytes 393224 | tf_op jit(solution)/shard_map/ppermute | solution.py:159
  49.1 34.8 %all-to-all-start.1 = ((f32[8,256,128]{2,1,0:T(8,128)}), f32[8,256,128]{2,1,0:T(8,128)S(1)}, u32[]{:S(2)}, u32[]{:S(2)}) async-start(f32[8,256,128]{2,1,0:T(8,128)} %broadcast_in_dim.7), calls=%async_computation.1 | async-start | bytes 2097152 | tf_op jit(solution)/shard_map/all_to_all | solution.py:182
  56.0 60.1 %all-gather.3.cloned.1.call-start = ((), (), s32[]{:S(2)}) async-start(), calls=%async_computation.2 | async-start | bytes 1179648 | tf_op jit(solution)/shard_map/all_gather | solution.py:192
  56.0 5.5 %collective-permute-start = (f32[128,256]{1,0:T(8,128)S(1)}, f32[128,256]{1,0:T(8,128)S(1)}, u32[]{:S(2)}, u32[]{:S(2)}) collective-permute-start(f32[128,256]{1,0:T(8,128)S(1)} %bitcast.15), channel_id=1, source_target_pairs={{0,384},{1,385},{2,386},{3,387},{4,388},{5,389},{6,390},{7,391},{8... | collective-permute-start | bytes 393224 | tf_op jit(solution)/shard_map/ppermute | solution.py:159
  57.3 4.2 %collective-permute-start.1 = (f32[128,256]{1,0:T(8,128)S(1)}, f32[128,256]{1,0:T(8,128)S(1)}, u32[]{:S(2)}, u32[]{:S(2)}) collective-permute-start(f32[128,256]{1,0:T(8,128)S(1)} %bitcast.16), channel_id=1, source_target_pairs={{0,256},{1,257},{2,258},{3,259},{4,260},{5,261},{6,262},{7,263},{8... | collective-permute-start | bytes 393224 | tf_op jit(solution)/shard_map/ppermute | solution.py:159
  59.5 4.2 %collective-permute-start.2 = (f32[128,256]{1,0:T(8,128)S(1)}, f32[128,256]{1,0:T(8,128)S(1)}, u32[]{:S(2)}, u32[]{:S(2)}) collective-permute-start(f32[128,256]{1,0:T(8,128)S(1)} %bitcast.17), channel_id=1, source_target_pairs={{0,128},{1,129},{2,130},{3,131},{4,132},{5,133},{6,134},{7,135},{8... | collective-permute-start | bytes 393224 | tf_op jit(solution)/shard_map/ppermute | solution.py:159
  84.0 4.9 %collective-permute-start.7 = (f32[6,256,128]{2,1,0:T(8,128)S(1)}, f32[6,256,128]{2,1,0:T(8,128)S(1)}, u32[]{:S(2)}, u32[]{:S(2)}) collective-permute-start(f32[6,256,128]{2,1,0:T(8,128)S(1)} %slice.20.near), channel_id=1, source_target_pairs={{0,1},{1,0},{2,3},{3,2},{4,5},{5,4},{6,7},{7,6},{8,9},{9,8},{10,11... | collective-permute-start | bytes 2359304 | tf_op jit(solution)/shard_map/ppermute | solution.py:159
  87.0 29.1 %collective-permute-start.3 = (f32[3,128,128]{2,1,0:T(8,128)S(1)}, f32[3,128,128]{2,1,0:T(8,128)S(1)}, u32[]{:S(2)}, u32[]{:S(2)}) collective-permute-start(f32[3,128,128]{2,1,0:T(8,128)S(1)} %slice.18.near), channel_id=1, source_target_pairs={{0,1},{1,0},{2,3},{3,2},{4,5},{5,4},{6,7},{7,6},{8,9},{9,8},{10,11... | collective-permute-start | bytes 589832 | tf_op jit(solution)/shard_map/ppermute | solution.py:159
  116.1 1.2 copy-start
Sparse Core Ops, SparseCore 0:
  64.5 37.0 all-gather.2

commit v3 on v2

--- a/solution.py
+++ b/solution.py
@@ -8,6 +8,7 @@
 TILE = 128
 NB = 6
 GROUP = 32
+WINDOW = 16
 XS, YS, ZS = 4, 8, 8
 ZSRC = NB // 2
 VMEM_LIMIT = 48 * 1024 * 1024
@@ -29,41 +30,53 @@
 def eliminate(rows, offset):
     count, width = rows.shape
     groups = count // 8
-    wide = width // TILE
-    block = rows[:, offset : offset + count]
-    column = {}
-    for j in range(count):
-        for g in range(j // 8, groups):
-            column[g, j] = jnp.broadcast_to(block[8 * g : 8 * g + 8, j : j + 1], (8, TILE))
+
+    def wide(value):
+        return jnp.concatenate([value] * (width // TILE), axis=1)
+
     part = [rows[8 * g : 8 * g + 8] for g in range(groups)]
     sublane = lax.broadcasted_iota(jnp.int32, (8, TILE), 0)
     scale = [None] * groups
-    for k in range(count):
-        gk, sk = divmod(k, 8)
-        pivot = spread(column[gk, k][sk : sk + 1])
-        inverse = pl.reciprocal(pivot)
-        root = lax.rsqrt(pivot)
-        scale[gk] = root if scale[gk] is None else jnp.where(sublane == sk, root, scale[gk])
-        factor = {}
-        for g in range(gk, groups):
-            value = column[g, k] * inverse
-            factor[g] = jnp.where(sublane > sk, value, 0.0) if g == gk else value
-        for j in range(k + 1, count):
-            gj, sj = divmod(j, 8)
-            across = spread(column[gj, k][sj : sj + 1])
-            for g in range(gj, groups):
-                column[g, j] = column[g, j] - factor[g] * across
-        pivot_row = spread(part[gk][sk : sk + 1])
-        for g in range(gk, groups):
-            if g == gk and sk == 7:
-                continue
-            part[g] = part[g] - jnp.concatenate([factor[g]] * wide, axis=1) * pivot_row
-    return jnp.concatenate(
-        [part[g] * jnp.concatenate([scale[g]] * wide, axis=1) for g in range(groups)], axis=0
-    )
-
-
-def factor_tile(tile):
+    for start in range(0, count, WINDOW):
+        column = {}
+        for j in range(start, start + WINDOW):
+            for g in range(j // 8, groups):
+                lane = offset + j
+                column[g, j] = jnp.broadcast_to(part[g][:, lane : lane + 1], (8, TILE))
+        for k in range(start, start + WINDOW, 2):
+            gk, sk = divmod(k, 8)
+            first = spread(column[gk, k][sk : sk + 1])
+            cross = spread(column[gk, k][sk + 1 : sk + 2])
+            second = spread(column[gk, k + 1][sk + 1 : sk + 2])
+            determinant = first * second - cross * cross
+            inverse = pl.reciprocal(determinant)
+            factor = {}
+            for g in range(gk, groups):
+                a, b = column[g, k], column[g, k + 1]
+                both = [(a * second - b * cross) * inverse, (b * first - a * cross) * inverse]
+                if g == gk:
+                    both = [jnp.where(sublane > sk + 1, value, 0.0) for value in both]
+                factor[g] = both
+            for j in range(k + 2, start + WINDOW):
+                gj, sj = divmod(j, 8)
+                across = [spread(column[gj, k + i][sj : sj + 1]) for i in range(2)]
+                for g in range(gj, groups):
+                    column[g, j] = column[g, j] - (factor[g][0] * across[0] + factor[g][1] * across[1])
+            pivot_rows = [spread(part[gk][sk + i : sk + i + 1]) for i in range(2)]
+            reciprocal = pl.reciprocal(first)
+            roots = [lax.rsqrt(first), lax.rsqrt(determinant * reciprocal)]
+            own = jnp.where(sublane == sk, roots[0], jnp.where(sublane == sk + 1, roots[1], 1.0))
+            scale[gk] = own if scale[gk] is None else scale[gk] * own
+            inside = jnp.where(sublane == sk + 1, cross * reciprocal, 0.0)
+            for g in range(gk, groups):
+                taken = wide(factor[g][0]) * pivot_rows[0] + wide(factor[g][1]) * pivot_rows[1]
+                if g == gk:
+                    taken = taken + wide(inside) * pivot_rows[0]
+                part[g] = part[g] - taken
+    return jnp.concatenate([part[g] * wide(scale[g]) for g in range(groups)], axis=0)
+
+
+def factor_tile(tile, beside):
     row = lax.broadcasted_iota(jnp.int32, (TILE, TILE), 0)
     lane = lax.broadcasted_iota(jnp.int32, (TILE, TILE), 1)
     both = jnp.concatenate([tile, jnp.where(row == lane, 1.0, 0.0)], axis=1)
@@ -74,7 +87,9 @@
             rows = rows - dot_t(upper[:, start : start + GROUP], upper)
         rows = eliminate(rows, start)
         upper = rows if upper is None else jnp.concatenate([upper, rows], axis=0)
-    return upper[:, :TILE], upper[:, TILE:]
+        for task in beside[start // GROUP :: TILE // GROUP]:
+            task()
+    return upper[:, TILE:]
 
 
 def dot_nt(a, b):
@@ -84,16 +99,14 @@
 def factor_kernel(place, near, far, inverse, upper):
     core = place[2]
 
-    def place_tiles(source, shift):
+    def place_tiles(source, parity):
         for i in range(NB):
-            if (i + shift) % 2 != place_tiles.parity:
-                continue
             for half in range(2):
-                distance = shift + 2 * half
+                distance = (i + parity) % 2 + 2 * half
                 j = (i + distance) % NB
                 if distance == NB // 2 and i >= NB // 2:
                     continue
-                tile = source[i, half * TILE : (half + 1) * TILE, :]
+                tile = jnp.concatenate([source[2 * half, i], source[2 * half + 1, i]], axis=0)
                 if i <= j:
                     upper[i * TILE : (i + 1) * TILE, j * TILE : (j + 1) * TILE] = tile
                 else:
@@ -103,23 +116,50 @@
 
         @pl.when(core == parity)
         def _():
-            for source, held in ((near, parity), (far, 1 - parity)):
-                place_tiles.parity = held
-                place_tiles(source, 0)
-                place_tiles(source, 1)
-
+            place_tiles(near, parity)
+            place_tiles(far, 1 - parity)
+
+    def at(i):
+        return slice(i * TILE, (i + 1) * TILE)
+
+    own, corner = [], None
     for b in range(NB):
-        lo, hi = b * TILE, (b + 1) * TILE
-        rows = upper[lo:hi, lo:]
+        tile = upper[at(b), at(b)]
         if b:
-            rows = rows - dot_t(upper[:lo, lo:hi], upper[:lo, lo:])
-        _, own = factor_tile(rows[:, :TILE])
-        inverse[lo:hi, lo:hi] = own
-        if hi < NB * TILE:
-            upper[lo:hi, hi:] = dot(own, rows[:, TILE:])
-            inverse[lo:hi, hi:] = jnp.zeros((TILE, NB * TILE - hi), jnp.float32)
+            tile = tile - dot_t(corner, corner)
+        beside = []
         if b:
-            inverse[lo:hi, :lo] = -dot(own, dot_t(upper[:lo, lo:hi], inverse[:lo, :lo]))
+            last = b - 1
+
+            def finish_row():
+                if b + 1 < NB:
+                    upper[at(last), (b + 1) * TILE :] = dot(own[last], upper[at(last), (b + 1) * TILE :])
+
+            def finish_inverse():
+                inverse[at(last), at(last)] = own[last]
+                inverse[at(last), b * TILE :] = jnp.zeros((TILE, (NB - b) * TILE), jnp.float32)
+                if last:
+                    inverse[at(last), : last * TILE] = -dot(own[last], inverse[at(last), : last * TILE])
+
+            def next_row():
+                if b + 1 < NB:
+                    upper[at(b), (b + 1) * TILE :] = upper[at(b), (b + 1) * TILE :] - dot_t(
+                        upper[: b * TILE, at(b)], upper[: b * TILE, (b + 1) * TILE :]
+                    )
+                    across = upper[: b * TILE, at(b + 1)]
+                    upper[at(b + 1), at(b + 1)] = upper[at(b + 1), at(b + 1)] - dot_t(across, across)
+
+            def next_inverse():
+                inverse[at(b), : b * TILE] = dot_t(upper[: b * TILE, at(b)], inverse[: b * TILE, : b * TILE])
+
+            beside = [finish_row, finish_inverse, next_row, next_inverse]
+        own.append(factor_tile(tile, beside))
+        if b + 1 < NB:
+            corner = dot(own[b], upper[at(b), at(b + 1)])
+            upper[at(b), at(b + 1)] = corner
+    last = NB - 1
+    inverse[at(last), at(last)] = own[last]
+    inverse[at(last), : last * TILE] = -dot(own[last], inverse[at(last), : last * TILE])
 
 
 def update_kernel(place, mine, strip, near, far, inverse, out, row_strip, solved):
@@ -165,15 +205,19 @@
 
 CHIPS = [(x, y) for x in range(XS) for y in range(YS)]
 COLUMNS = [(z, core) for z in range(ZS) for core in range(2)]
+X_GROUPS = [[x * YS + y for x in range(XS)] for y in range(YS)]
 Y_GROUPS = [[x * YS + y for y in range(YS)] for x in range(XS)]
 Z_GROUPS = [[z * 2 + core for z in range(ZS)] for core in range(2)]
+
+
+def x_pairs(step):
+    return [(device(0, y, *col), device(step, y, *col)) for y in range(NB) for col in COLUMNS]
 
 
 def along_x(array, x):
     result = array
     for step in range(1, XS):
-        pairs = [(device(0, y, *col), device(step, y, *col)) for y in range(NB) for col in COLUMNS]
-        result = jnp.where(x == step, send(array, pairs), result)
+        result = jnp.where(x == step, send(array, x_pairs(step)), result)
     return result
 
 
@@ -189,15 +233,19 @@
     x = row_tile // YS
     core = col_tile % 2
 
-    strip = lax.all_gather(along_x(block, x), "row", axis_index_groups=Y_GROUPS)
-
     near_row = to_all(block[:, :TILE], "col", Z_GROUPS)[:ZSRC]
+
+    near_row, pieces = lax.optimization_barrier((near_row, along_x(block, x)))
+    strip = lax.all_gather(pieces, "row", axis_index_groups=Y_GROUPS)
 
     first = jnp.where(row_tile % 2 == core, row_tile, (row_tile + 1) % NB)
     start = jnp.clip((first - core) // 2, 0, ZSRC - 1)
     wrapped = jnp.concatenate([near_row, near_row[:1]], axis=0)
-    tiles = lax.dynamic_slice_in_dim(wrapped, start, 2, 0).reshape(2 * TILE, TILE)
-    near = to_all(along_x(tiles, x), "row", Y_GROUPS)[:NB]
+    tiles = lax.dynamic_slice_in_dim(wrapped, start, 2, 0).reshape(XS, 2 * TILE // XS, TILE)
+    quarter = tiles[0]
+    for step in range(1, XS):
+        quarter = jnp.where(x == step, send(tiles[step], x_pairs(step)), quarter)
+    near = to_all(to_all(quarter, "row", Y_GROUPS)[:NB], "row", X_GROUPS)
 
     swap = [(device(*chip, z, c), device(*chip, z, 1 - c)) for chip in CHIPS for z, c in COLUMNS]
     far = send(near, swap)
@@ -215,7 +263,7 @@
         out_specs=vmem,
         scratch_shapes=[pltpu.VMEM((order, order), jnp.float32)],
         compiler_params=params,
-        cost_estimate=pl.CostEstimate(flops=4 * 10**9, bytes_accessed=8 * 10**6, transcendentals=0),
+        cost_estimate=pl.CostEstimate(flops=1, bytes_accessed=1, transcendentals=0),
     )(place, near, far)
     result = pl.pallas_call(
         update_kernel,

time: 132 us -> 120 us (0.909); the launches traced: 130 us -> 120 us
  waiting for transfers between devices: 43.6 us -> 20 us
  blocking collectives: 0 us -> 10.8 us
  starting transfers between devices: 35 us -> 40.5 us
  Pallas kernels: 32.2 us -> 28.5 us
    all_to_all x2, waiting for transfers between devices: 37.5 us -> 15.1 us  [to_all(): return lax.all_to_all(copies, axis, 0, 0, axis_index_groups=groups)]
    all_to_all x0 -> x1, blocking collectives: none -> 10.8 us  [to_all(): return lax.all_to_all(copies, axis, 0, 0, axis_index_groups=groups)]
    ppermute x8, starting transfers between devices: 17.2 us -> 22.8 us  [send(): return lax.ppermute(array, ('row', 'col'), pairs)]
    pallas_call x1, Pallas kernels: 27.1 us -> 23.6 us  [per_device(): pl.pallas_call(factor_kernel, out_shape=jax.ShapeDtypeStruct((order, orde...]
    ppermute x8, waiting for transfers between devices: 6.06 us -> 4.23 us  [send(): return lax.ppermute(array, ('row', 'col'), pairs)]
  transfers between devices with their start and end apart: 11 -> 11, of which waited for: 5 -> 5; matrix products, arithmetic and copies ran while one was open for 1% -> 1% of each run, Pallas kernels for 21% -> 20%
where the time goes in v3:
time: 120 us
  starting transfers between devices  40.5 us (34%)
  Pallas kernels  28.5 us (24%)
  waiting for transfers between devices  20 us (17%)
  between operations  13.7 us (11%)
  blocking collectives  10.8 us (9%)
  local copies, waits for them, and re-layouts  4.55 us (4%)
  other arithmetic  1.7 us (1%)
    pallas_call x1, Pallas kernels, per_device(): pl.pallas_call(factor_kernel, out_shape=jax.ShapeDtypeStruct((order, orde...  23.6 us
    ppermute x8, starting transfers between devices, send(): return lax.ppermute(array, ('row', 'col'), pairs)  22.8 us
    all_to_all x2, starting transfers between devices, to_all(): return lax.all_to_all(copies, axis, 0, 0, axis_index_groups=groups)  17.7 us
    all_to_all x2, waiting for transfers between devices, to_all(): return lax.all_to_all(copies, axis, 0, 0, axis_index_groups=groups)  15.1 us
    all_to_all x1, blocking collectives, to_all(): return lax.all_to_all(copies, axis, 0, 0, axis_index_groups=groups)  10.8 us
    pallas_call x1, Pallas kernels, per_device(): pl.pallas_call(update_kernel, out_shape=jax.ShapeDtypeStruct(block.shape,...  4.88 us
    ppermute x8, waiting for transfers between devices, send(): return lax.ppermute(array, ('row', 'col'), pairs)  4.23 us
  transfers between devices with their start and end apart: 11, of which 5 were waited for; matrix products, arithmetic and copies ran while one was open for 1% of the time, Pallas kernels for 20%

profile of v3, /device:TPU:1, one launch (start us, length us, event | category | flops | bytes accessed | tf_op | source)
XLA Modules:
  0.0 119.8 jit_solution(8529941716400467705)
XLA Ops:
  6.5 0.9 copy.6
  7.5 0.8 broadcast_in_dim.9
  8.3 10.9 %all-to-all-start = ((f32[8,128,128]{2,1,0:T(8,128)}), f32[8,128,128]{2,1,0:T(8,128)S(1)}, u32[]{:S(2)}, u32[]{:S(2)}) async-start(f32[8,128,128]{2,1,0:T(8,128)} %broadcast_in_dim.9), calls=%async_computation | async-start | bytes 1048576 | tf_op jit(solution)/shard_map/all_to_all | solution.py:226
  19.2 4.4 %collective-permute-start = (f32[128,256]{1,0:T(8,128)S(1)}, f32[128,256]{1,0:T(8,128)S(1)}, u32[]{:S(2)}, u32[]{:S(2)}) collective-permute-start(f32[128,256]{1,0:T(8,128)S(1)} %bitcast.28), channel_id=1, source_target_pairs={{0,384},{1,385},{2,386},{3,387},{4,388},{5,389},{6,390},{7,391},{8... | collective-permute-start | bytes 393224 | tf_op jit(solution)/shard_map/ppermute | solution.py:199
  23.5 1.3 %collective-permute-start.1 = (f32[128,256]{1,0:T(8,128)S(1)}, f32[128,256]{1,0:T(8,128)S(1)}, u32[]{:S(2)}, u32[]{:S(2)}) collective-permute-start(f32[128,256]{1,0:T(8,128)S(1)} %bitcast.29), channel_id=1, source_target_pairs={{0,256},{1,257},{2,258},{3,259},{4,260},{5,261},{6,262},{7,263},{8... | collective-permute-start | bytes 393224 | tf_op jit(solution)/shard_map/ppermute | solution.py:199
  24.9 1.3 %collective-permute-start.2 = (f32[128,256]{1,0:T(8,128)S(1)}, f32[128,256]{1,0:T(8,128)S(1)}, u32[]{:S(2)}, u32[]{:S(2)}) collective-permute-start(f32[128,256]{1,0:T(8,128)S(1)} %bitcast.30), channel_id=1, source_target_pairs={{0,128},{1,129},{2,130},{3,131},{4,132},{5,133},{6,134},{7,135},{8... | collective-permute-start | bytes 393224 | tf_op jit(solution)/shard_map/ppermute | solution.py:199
  26.2 0.0 collective-permute-done
  26.2 0.5 collective-permute-done.1
  26.8 2.7 %collective-permute-done.2 = f32[128,256]{1,0:T(8,128)S(1)} collective-permute-done((f32[128,256]{1,0:T(8,128)S(1)}, f32[128,256]{1,0:T(8,128)S(1)}, u32[]{:S(2)}, u32[]{:S(2)}) %collective-permute-start.2) | collective-permute-done | bytes 131104 | tf_op jit(solution)/shard_map/ppermute | solution.py:199
  29.5 1.6 %select_select_fusion = f32[128,256]{1,0:T(8,128)} fusion(f32[128,256]{1,0:T(8,128)S(1)} %collective-permute-done, f32[128,256]{1,0:T(8,128)S(1)} %collective-permute-done.1, f32[128,256]{1,0:T(8,128)S(1)} %collective-permute-done.2, pred[]{:T(512)S(6)} %eq.21, pred[]{:T(512)S(6)} %eq.20, pred[]{:T(512)S(6)} %eq.19, f32[16,8,2,128]{3,2,1,0:T(2,128)} %bitcast.35), kind=kLoop, calls=%fused_computation.4 | loop fusion | flops 98304 | bytes 655363 | tf_op jit(solution)/shard_map/jit(_where)/select_n | solution.py:220
  31.1 6.0 %all-to-all-done = f32[8,128,128]{2,1,0:T(8,128)S(1)} async-done(((f32[8,128,128]{2,1,0:T(8,128)}), f32[8,128,128]{2,1,0:T(8,128)S(1)}, u32[]{:S(2)}, u32[]{:S(2)}) %all-to-all-start) | async-done | bytes 524320 | tf_op jit(solution)/shard_map/all_to_all | solution.py:226
  37.2 4.4 %collective-permute-start.4 = (f32[64,128]{1,0:T(8,128)S(1)}, f32[64,128]{1,0:T(8,128)S(1)}, u32[]{:S(2)}, u32[]{:S(2)}) collective-permute-start(f32[64,128]{1,0:T(8,128)S(1)} %get-tuple-element.11), channel_id=1, source_target_pairs={{0,384},{1,385},{2,386},{3,387},{4,388},{5,389},{6,390},{7,391},{8... | collective-permute-start | bytes 98312 | tf_op jit(solution)/shard_map/ppermute | solution.py:199
  41.6 1.3 %collective-permute-start.5 = (f32[64,128]{1,0:T(8,128)S(1)}, f32[64,128]{1,0:T(8,128)S(1)}, u32[]{:S(2)}, u32[]{:S(2)}) collective-permute-start(f32[64,128]{1,0:T(8,128)S(1)} %get-tuple-element.10), channel_id=1, source_target_pairs={{0,256},{1,257},{2,258},{3,259},{4,260},{5,261},{6,262},{7,263},{8... | collective-permute-start | bytes 98312 | tf_op jit(solution)/shard_map/ppermute | solution.py:199
  42.9 1.3 %collective-permute-start.6 = (f32[64,128]{1,0:T(8,128)S(1)}, f32[64,128]{1,0:T(8,128)S(1)}, u32[]{:S(2)}, u32[]{:S(2)}) collective-permute-start(f32[64,128]{1,0:T(8,128)S(1)} %get-tuple-element.9), channel_id=1, source_target_pairs={{0,128},{1,129},{2,130},{3,131},{4,132},{5,133},{6,134},{7,135},{8... | collective-permute-start | bytes 98312 | tf_op jit(solution)/shard_map/ppermute | solution.py:199
  44.2 0.0 collective-permute-done.4
  44.2 0.0 collective-permute-done.5
  44.2 1.0 collective-permute-done.6
  45.2 0.7 broadcast_in_dim.10
  46.0 6.8 %all-to-all-start.1 = ((f32[8,64,128]{2,1,0:T(8,128)}), f32[8,64,128]{2,1,0:T(8,128)S(1)}, u32[]{:S(2)}, u32[]{:S(2)}) async-start(f32[8,64,128]{2,1,0:T(8,128)} %broadcast_in_dim.10), calls=%async_computation.1 | async-start | bytes 524288 | tf_op jit(solution)/shard_map/all_to_all | solution.py:226
  52.8 0.0 all-gather.3.cloned.1.call-start
  52.8 0.7 all-gather.3.cloned.1.call-update
  53.5 9.0 %all-to-all-done.1 = f32[8,64,128]{2,1,0:T(8,128)S(1)} async-done(((f32[8,64,128]{2,1,0:T(8,128)}), f32[8,64,128]{2,1,0:T(8,128)S(1)}, u32[]{:S(2)}, u32[]{:S(2)}) %all-to-all-start.1) | async-done | bytes 262176 | tf_op jit(solution)/shard_map/all_to_all | solution.py:226
  62.6 0.1 broadcast_in_dim.11
  62.7 10.8 %all_to_all.15.near = f32[4,6,64,128]{3,2,1,0:T(8,128)S(1)} all-to-all(f32[4,6,64,128]{3,2,1,0:T(8,128)S(1)} %broadcast_in_dim.11), channel_id=1, replica_groups={{0,128,256,384},{16,144,272,400},{32,160,288,416},{48,176,304,432},{64,..., dimensions={0} | all-to-all | bytes 1572864 | tf_op jit(solution)/shard_map/all_to_all | solution.py:226
  73.4 7.0 %collective-permute-start.7 = (f32[4,6,64,128]{3,2,1,0:T(8,128)S(1)}, f32[4,6,64,128]{3,2,1,0:T(8,128)S(1)}, u32[]{:S(2)}, u32[]{:S(2)}) collective-permute-start(f32[4,6,64,128]{3,2,1,0:T(8,128)S(1)} %all_to_all.15.near), channel_id=1, source_target_pairs={{0,1},{1,0},{2,3},{3,2},{4,5},{5,4},{6,7},{7,6},{8,9},{9,8},{10,11... | collective-permute-start | bytes 2359304 | tf_op jit(solution)/shard_map/ppermute | solution.py:199
  80.4 1.9 %collective-permute-start.3 = (f32[3,128,128]{2,1,0:T(8,128)S(1)}, f32[3,128,128]{2,1,0:T(8,128)S(1)}, u32[]{:S(2)}, u32[]{:S(2)}) collective-permute-start(f32[3,128,128]{2,1,0:T(8,128)S(1)} %slice.33.near), channel_id=1, source_target_pairs={{0,1},{1,0},{2,3},{3,2},{4,5},{5,4},{6,7},{7,6},{8,9},{9,8},{10,11... | collective-permute-start | bytes 589832 | tf_op jit(solution)/shard_map/ppermute | solution.py:199
  82.3 0.1 pad_add_fusion.place
  82.4 23.6 %shard_map.17.inverse = f32[768,768]{1,0:T(8,128)S(1)} custom-call(s32[3]{0:T(128)S(1)} %pad_add_fusion.place, f32[4,6,64,128]{3,2,1,0:T(8,128)S(1)} %all_to_all.15.near, f32[4,6,64,128]{3,2,1,0:T(8,128)S(1)} %collective-permute-done.7.far), custom_call_target="tpu_custom_call" | custom-call | flops 1 | bytes 1 | tf_op jit(solution)/shard_map/pallas_call | solution.py:259
  106.1 0.0 all-gather.3.cloned.1.call-done
  106.1 1.2 %copy-done = f32[1024,256]{1,0:T(8,128)S(1)} copy-done((f32[1024,256]{1,0:T(8,128)S(1)}, f32[1024,256]{1,0:T(8,128)}, u32[]{:S(2)}) %copy-start) | copy-done | bytes 1048600
  107.3 4.9 %shard_map.18 = f32[128,256]{1,0:T(8,128)S(1)} custom-call(s32[3]{0:T(128)S(1)} %pad_add_fusion.place, f32[128,256]{1,0:T(8,128)S(1)} %bitcast.31, f32[8,128,256]{2,1,0:T(8,128)S(1)} %bitcast.26, f32[3,128,128]{2,1,0:T(8,128)S(1)} %slice.33.near, f32[3,128,128]{2,1,0:T(8,128)S(1)} %collective-permute-done.3.far, f32[768,768]{1,0:T(8,128)S(1)} %shard_map.17.inverse), custom_call_target="tpu_custom_call" | custom-call | tf_op jit(solution)/shard_map/pallas_call | solution.py:268
  112.2 0.7 reshape.11
  (10 shorter events, 0.1 us)
Async XLA Ops:
  8.3 28.8 %all-to-all-start = ((f32[8,128,128]{2,1,0:T(8,128)}), f32[8,128,128]{2,1,0:T(8,128)S(1)}, u32[]{:S(2)}, u32[]{:S(2)}) async-start(f32[8,128,128]{2,1,0:T(8,128)} %broadcast_in_dim.9), calls=%async_computation | async-start | bytes 1048576 | tf_op jit(solution)/shard_map/all_to_all | solution.py:226
  19.2 7.1 %collective-permute-start = (f32[128,256]{1,0:T(8,128)S(1)}, f32[128,256]{1,0:T(8,128)S(1)}, u32[]{:S(2)}, u32[]{:S(2)}) collective-permute-start(f32[128,256]{1,0:T(8,128)S(1)} %bitcast.28), channel_id=1, source_target_pairs={{0,384},{1,385},{2,386},{3,387},{4,388},{5,389},{6,390},{7,391},{8... | collective-permute-start | bytes 393224 | tf_op jit(solution)/shard_map/ppermute | solution.py:199
  23.5 3.2 %collective-permute-start.1 = (f32[128,256]{1,0:T(8,128)S(1)}, f32[128,256]{1,0:T(8,128)S(1)}, u32[]{:S(2)}, u32[]{:S(2)}) collective-permute-start(f32[128,256]{1,0:T(8,128)S(1)} %bitcast.29), channel_id=1, source_target_pairs={{0,256},{1,257},{2,258},{3,259},{4,260},{5,261},{6,262},{7,263},{8... | collective-permute-start | bytes 393224 | tf_op jit(solution)/shard_map/ppermute | solution.py:199
  24.9 4.6 %collective-permute-start.2 = (f32[128,256]{1,0:T(8,128)S(1)}, f32[128,256]{1,0:T(8,128)S(1)}, u32[]{:S(2)}, u32[]{:S(2)}) collective-permute-start(f32[128,256]{1,0:T(8,128)S(1)} %bitcast.30), channel_id=1, source_target_pairs={{0,128},{1,129},{2,130},{3,131},{4,132},{5,133},{6,134},{7,135},{8... | collective-permute-start | bytes 393224 | tf_op jit(solution)/shard_map/ppermute | solution.py:199
  37.2 7.0 %collective-permute-start.4 = (f32[64,128]{1,0:T(8,128)S(1)}, f32[64,128]{1,0:T(8,128)S(1)}, u32[]{:S(2)}, u32[]{:S(2)}) collective-permute-start(f32[64,128]{1,0:T(8,128)S(1)} %get-tuple-element.11), channel_id=1, source_target_pairs={{0,384},{1,385},{2,386},{3,387},{4,388},{5,389},{6,390},{7,391},{8... | collective-permute-start | bytes 98312 | tf_op jit(solution)/shard_map/ppermute | solution.py:199
  41.6 2.6 %collective-permute-start.5 = (f32[64,128]{1,0:T(8,128)S(1)}, f32[64,128]{1,0:T(8,128)S(1)}, u32[]{:S(2)}, u32[]{:S(2)}) collective-permute-start(f32[64,128]{1,0:T(8,128)S(1)} %get-tuple-element.10), channel_id=1, source_target_pairs={{0,256},{1,257},{2,258},{3,259},{4,260},{5,261},{6,262},{7,263},{8... | collective-permute-start | bytes 98312 | tf_op jit(solution)/shard_map/ppermute | solution.py:199
  42.9 2.3 %collective-permute-start.6 = (f32[64,128]{1,0:T(8,128)S(1)}, f32[64,128]{1,0:T(8,128)S(1)}, u32[]{:S(2)}, u32[]{:S(2)}) collective-permute-start(f32[64,128]{1,0:T(8,128)S(1)} %get-tuple-element.9), channel_id=1, source_target_pairs={{0,128},{1,129},{2,130},{3,131},{4,132},{5,133},{6,134},{7,135},{8... | collective-permute-start | bytes 98312 | tf_op jit(solution)/shard_map/ppermute | solution.py:199
  46.0 16.6 %all-to-all-start.1 = ((f32[8,64,128]{2,1,0:T(8,128)}), f32[8,64,128]{2,1,0:T(8,128)S(1)}, u32[]{:S(2)}, u32[]{:S(2)}) async-start(f32[8,64,128]{2,1,0:T(8,128)} %broadcast_in_dim.10), calls=%async_computation.1 | async-start | bytes 524288 | tf_op jit(solution)/shard_map/all_to_all | solution.py:226
  52.8 53.3 %all-gather.3.cloned.1.call-start = ((), (), s32[]{:S(2)}) async-start(), calls=%async_computation.3 | async-start | bytes 1179648 | tf_op jit(solution)/shard_map/all_gather | solution.py:239
  73.4 9.0 %collective-permute-start.7 = (f32[4,6,64,128]{3,2,1,0:T(8,128)S(1)}, f32[4,6,64,128]{3,2,1,0:T(8,128)S(1)}, u32[]{:S(2)}, u32[]{:S(2)}) collective-permute-start(f32[4,6,64,128]{3,2,1,0:T(8,128)S(1)} %all_to_all.15.near), channel_id=1, source_target_pairs={{0,1},{1,0},{2,3},{3,2},{4,5},{5,4},{6,7},{7,6},{8,9},{9,8},{10,11... | collective-permute-start | bytes 2359304 | tf_op jit(solution)/shard_map/ppermute | solution.py:199
  80.4 25.7 %collective-permute-start.3 = (f32[3,128,128]{2,1,0:T(8,128)S(1)}, f32[3,128,128]{2,1,0:T(8,128)S(1)}, u32[]{:S(2)}, u32[]{:S(2)}) collective-permute-start(f32[3,128,128]{2,1,0:T(8,128)S(1)} %slice.33.near), channel_id=1, source_target_pairs={{0,1},{1,0},{2,3},{3,2},{4,5},{5,4},{6,7},{7,6},{8,9},{9,8},{10,11... | collective-permute-start | bytes 589832 | tf_op jit(solution)/shard_map/ppermute | solution.py:199
  106.1 1.2 %copy-start = (f32[1024,256]{1,0:T(8,128)S(1)}, f32[1024,256]{1,0:T(8,128)}, u32[]{:S(2)}) copy-start(f32[1024,256]{1,0:T(8,128)} %all-gather.3.cloned.1.call-done) | copy-start | bytes 3145732
Sparse Core Ops, SparseCore 0:
  55.7 33.1 all-gather.2

commit v4 on v3

--- a/solution.py
+++ b/solution.py
@@ -10,6 +10,7 @@
 GROUP = 32
 WINDOW = 16
 XS, YS, ZS = 4, 8, 8
+SENT = NB // 2 + 1
 ZSRC = NB // 2
 VMEM_LIMIT = 48 * 1024 * 1024
 HI = lax.Precision.HIGHEST
@@ -53,15 +54,21 @@
             factor = {}
             for g in range(gk, groups):
                 a, b = column[g, k], column[g, k + 1]
-                both = [(a * second - b * cross) * inverse, (b * first - a * cross) * inverse]
-                if g == gk:
-                    both = [jnp.where(sublane > sk + 1, value, 0.0) for value in both]
-                factor[g] = both
-            for j in range(k + 2, start + WINDOW):
+                factor[g] = [a * second - b * cross, b * first - a * cross]
+            for j in range(k + 2, min(k + 4, start + WINDOW)):
+                gj, sj = divmod(j, 8)
+                across = [spread(column[gj, k + i][sj : sj + 1]) for i in range(2)]
+                for g in range(gj, groups):
+                    taken = factor[g][0] * across[0] + factor[g][1] * across[1]
+                    column[g, j] = column[g, j] - taken * inverse
+            for g in range(gk, groups):
+                factor[g] = [value * inverse for value in factor[g]]
+            for j in range(k + 4, start + WINDOW):
                 gj, sj = divmod(j, 8)
                 across = [spread(column[gj, k + i][sj : sj + 1]) for i in range(2)]
                 for g in range(gj, groups):
                     column[g, j] = column[g, j] - (factor[g][0] * across[0] + factor[g][1] * across[1])
+            factor[gk] = [jnp.where(sublane > sk + 1, value, 0.0) for value in factor[gk]]
             pivot_rows = [spread(part[gk][sk + i : sk + i + 1]) for i in range(2)]
             reciprocal = pl.reciprocal(first)
             roots = [lax.rsqrt(first), lax.rsqrt(determinant * reciprocal)]
@@ -84,10 +91,11 @@
     for start in range(0, TILE, GROUP):
         rows = both[start : start + GROUP]
         if upper is not None:
-            rows = rows - dot_t(upper[:, start : start + GROUP], upper)
+            rows = rows - dot(upper.T[start : start + GROUP], upper)
         rows = eliminate(rows, start)
         upper = rows if upper is None else jnp.concatenate([upper, rows], axis=0)
-        for task in beside[start // GROUP :: TILE // GROUP]:
+        slot, slots = start // GROUP, TILE // GROUP
+        for task in beside[slot * len(beside) // slots : (slot + 1) * len(beside) // slots]:
             task()
     return upper[:, TILE:]
 
@@ -96,38 +104,44 @@
     return lax.dot_general(a, b, (((1,), (1,)), ((), ())), precision=HI, preferred_element_type=jnp.float32)
 
 
-def factor_kernel(place, near, far, inverse, upper):
+def factor_kernel(place, near, far, near_row, far_row, panel, weights, upper, inverse):
     core = place[2]
 
-    def place_tiles(source, parity):
-        for i in range(NB):
-            for half in range(2):
-                distance = (i + parity) % 2 + 2 * half
+    def held(near_tile, far_tile, parity):
+        return jnp.where(core == parity, near_tile, far_tile)
+
+    def diagonal_tile(i, distance):
+        half, parity = distance // 2, (i + distance) % 2
+        parts = [held(near[2 * half + k, i], far[2 * half + k, i], parity) for k in range(2)]
+        return jnp.concatenate(parts, axis=0)
+
+    def place_row(i):
+        def task():
+            for distance in range(SENT if i < NB // 2 else SENT - 1):
                 j = (i + distance) % NB
-                if distance == NB // 2 and i >= NB // 2:
-                    continue
-                tile = jnp.concatenate([source[2 * half, i], source[2 * half + 1, i]], axis=0)
-                if i <= j:
-                    upper[i * TILE : (i + 1) * TILE, j * TILE : (j + 1) * TILE] = tile
-                else:
-                    upper[j * TILE : (j + 1) * TILE, i * TILE : (i + 1) * TILE] = tile.T
-
-    for parity in range(2):
-
-        @pl.when(core == parity)
-        def _():
-            place_tiles(near, parity)
-            place_tiles(far, 1 - parity)
+                if i < j:
+                    upper[at(i), at(j)] = diagonal_tile(i, distance)
+                elif i > j:
+                    upper[at(j), at(i)] = diagonal_tile(i, distance).T
+                elif i:
+                    upper[at(i), at(i)] = diagonal_tile(i, 0)
+
+        return task
+
+    def place_row_strip():
+        for j in range(NB):
+            panel[:, at(j)] = held(near_row[j // 2], far_row[j // 2], j % 2)
 
     def at(i):
         return slice(i * TILE, (i + 1) * TILE)
 
     own, corner = [], None
     for b in range(NB):
-        tile = upper[at(b), at(b)]
         if b:
-            tile = tile - dot_t(corner, corner)
-        beside = []
+            tile = upper[at(b), at(b)] - dot_t(corner, corner)
+        else:
+            tile = diagonal_tile(0, 0)
+            beside = [place_row(i) for i in range(NB)] + [place_row_strip]
         if b:
             last = b - 1
 
@@ -137,7 +151,8 @@
 
             def finish_inverse():
                 inverse[at(last), at(last)] = own[last]
-                inverse[at(last), b * TILE :] = jnp.zeros((TILE, (NB - b) * TILE), jnp.float32)
+                if b < NB - 1:
+                    inverse[at(last), b * TILE : (NB - 1) * TILE] = jnp.zeros((TILE, (NB - 1 - b) * TILE), jnp.float32)
                 if last:
                     inverse[at(last), : last * TILE] = -dot(own[last], inverse[at(last), : last * TILE])
 
@@ -152,39 +167,34 @@
             def next_inverse():
                 inverse[at(b), : b * TILE] = dot_t(upper[: b * TILE, at(b)], inverse[: b * TILE, : b * TILE])
 
-            beside = [finish_row, finish_inverse, next_row, next_inverse]
+            def panel_tile():
+                panel[:, at(last)] = dot_nt(panel[:, at(last)], own[last])
+                panel[:, at(b)] = panel[:, at(b)] - dot(panel[:, : b * TILE], upper[: b * TILE, at(b)])
+
+            def add_weights():
+                term = dot(panel[:, at(last)], inverse[at(last), : b * TILE])
+                if last:
+                    weights[:, : last * TILE] = weights[:, : last * TILE] + term[:, : last * TILE]
+                weights[:, at(last)] = term[:, last * TILE :]
+
+            beside = [finish_row, finish_inverse, next_row, next_inverse, panel_tile, add_weights]
         own.append(factor_tile(tile, beside))
         if b + 1 < NB:
             corner = dot(own[b], upper[at(b), at(b + 1)])
             upper[at(b), at(b + 1)] = corner
     last = NB - 1
-    inverse[at(last), at(last)] = own[last]
-    inverse[at(last), : last * TILE] = -dot(own[last], inverse[at(last), : last * TILE])
-
-
-def update_kernel(place, mine, strip, near, far, inverse, out, row_strip, solved):
-    row_tile, col_tile, core = place[0], place[1], place[2]
-
-    for parity in range(2):
-
-        @pl.when(core == parity)
-        def _():
-            for j in range(NB):
-                source = near if j % 2 == parity else far
-                row_strip[:, j * TILE : (j + 1) * TILE] = source[j // 2]
-
-    panel = []
-    for b in range(NB):
-        hi = (b + 1) * TILE
-        lower = inverse[b * TILE : hi, :hi]
-        total = None
-        for i in range(b + 1):
-            term = dot(lower[:, i * TILE : (i + 1) * TILE], strip[i])
-            total = term if total is None else total + term
-        solved[b * TILE : hi, :] = total
-        panel.append(dot_nt(row_strip[:, :hi], lower))
-    trailing = mine[...] - dot(jnp.concatenate(panel, axis=1), solved[...])
-    out[...] = jnp.where(row_tile >= NB, trailing, 0.0)
+    done = dot_nt(panel[:, at(last)], own[last])
+    panel[:, at(last)] = done
+    weights[:, at(last)] = dot(done, own[last])
+    left = dot(own[last], inverse[at(last), : last * TILE])
+    weights[:, : last * TILE] = weights[:, : last * TILE] - dot(done, left)
+
+
+def update_kernel(place, mine, strip, panel, weights, out):
+    row_tile, col_tile = place[0], place[1]
+    columns = strip[:NB].reshape(NB * TILE, 2 * TILE)
+    total = mine[...] - dot(weights[...], columns)
+    out[...] = jnp.where(row_tile >= NB, total, 0.0)
     row = lax.broadcasted_iota(jnp.int32, (TILE, TILE), 0)
     lane = lax.broadcasted_iota(jnp.int32, (TILE, TILE), 1)
     for j in range(NB):
@@ -192,7 +202,7 @@
         @pl.when(col_tile == j)
         def _():
             keep = row + (row_tile - j) * TILE >= lane
-            out[:, :TILE] = jnp.where(keep, panel[j], 0.0)
+            out[:, :TILE] = jnp.where(keep, panel[:, j * TILE : (j + 1) * TILE], 0.0)
 
 
 def send(array, pairs):
@@ -245,34 +255,33 @@
     quarter = tiles[0]
     for step in range(1, XS):
         quarter = jnp.where(x == step, send(tiles[step], x_pairs(step)), quarter)
-    near = to_all(to_all(quarter, "row", Y_GROUPS)[:NB], "row", X_GROUPS)
-
     swap = [(device(*chip, z, c), device(*chip, z, 1 - c)) for chip in CHIPS for z, c in COLUMNS]
+    far_row = send(near_row, swap)
+    tiles, far_row = lax.optimization_barrier((to_all(quarter, "row", Y_GROUPS)[:NB], far_row))
+    near = to_all(tiles, "row", X_GROUPS)
     far = send(near, swap)
-    far_row = send(near_row, swap)
 
     place = jnp.stack([row_tile, col_tile, core]).astype(jnp.int32)
     smem = pl.BlockSpec(memory_space=pltpu.SMEM)
     vmem = pl.BlockSpec(memory_space=pltpu.VMEM)
     params = pltpu.CompilerParams(vmem_limit_bytes=VMEM_LIMIT)
     order = NB * TILE
-    inverse = pl.pallas_call(
+    panel, weights = pl.pallas_call(
         factor_kernel,
-        out_shape=jax.ShapeDtypeStruct((order, order), jnp.float32),
-        in_specs=[smem, vmem, vmem],
-        out_specs=vmem,
-        scratch_shapes=[pltpu.VMEM((order, order), jnp.float32)],
+        out_shape=[jax.ShapeDtypeStruct((TILE, order), jnp.float32)] * 2,
+        in_specs=[smem, vmem, vmem, vmem, vmem],
+        out_specs=[vmem, vmem],
+        scratch_shapes=[pltpu.VMEM((order, order), jnp.float32)] * 2,
         compiler_params=params,
         cost_estimate=pl.CostEstimate(flops=1, bytes_accessed=1, transcendentals=0),
-    )(place, near, far)
+    )(place, near, far, near_row, far_row)
     result = pl.pallas_call(
         update_kernel,
         out_shape=jax.ShapeDtypeStruct(block.shape, jnp.float32),
-        in_specs=[smem, vmem, vmem, vmem, vmem, vmem],
+        in_specs=[smem, vmem, vmem, vmem, vmem],
         out_specs=vmem,
-        scratch_shapes=[pltpu.VMEM((TILE, order), jnp.float32), pltpu.VMEM((order, 2 * TILE), jnp.float32)],
         compiler_params=params,
-    )(place, block, strip, near_row, far_row, inverse)
+    )(place, block, strip, panel, weights)
     return result.reshape(matrix.shape)
 
 

time: 120 us -> 116 us (0.967)
  Pallas kernels: 28.5 us -> 24.6 us
  starting transfers between devices: 40.5 us -> 42.3 us
    pallas_call x1, Pallas kernels: 4.88 us -> 1.14 us  [per_device(): pl.pallas_call(update_kernel, out_shape=jax.ShapeDtypeStruct(block.shape,...]
    all_to_all x2, waiting for transfers between devices: 15.1 us -> 12.3 us  [to_all(): return lax.all_to_all(copies, axis, 0, 0, axis_index_groups=groups)]
    ppermute x8, waiting for transfers between devices: 4.23 us -> 6.04 us  [send(): return lax.ppermute(array, ('row', 'col'), pairs)]
    ppermute x8, starting transfers between devices: 22.8 us -> 24.6 us  [send(): return lax.ppermute(array, ('row', 'col'), pairs)]
  transfers between devices with their start and end apart: 11 -> 11, of which waited for: 5 -> 6; matrix products, arithmetic and copies ran while one was open for 1% -> 1% of each run, Pallas kernels for 20% -> 20%
where the time goes in v4:
time: 116 us
  starting transfers between devices  42.3 us (36%)
  Pallas kernels  24.6 us (21%)
  waiting for transfers between devices  19 us (16%)
  between operations  13.7 us (12%)
  blocking collectives  10.8 us (9%)
  local copies, waits for them, and re-layouts  4.55 us (4%)
    ppermute x8, starting transfers between devices, send(): return lax.ppermute(array, ('row', 'col'), pairs)  24.6 us
    pallas_call x1, Pallas kernels, per_device(): pl.pallas_call(factor_kernel, out_shape=[jax.ShapeDtypeStruct((TILE, orde...  23.4 us
    all_to_all x2, starting transfers between devices, to_all(): return lax.all_to_all(copies, axis, 0, 0, axis_index_groups=groups)  17.7 us
    all_to_all x2, waiting for transfers between devices, to_all(): return lax.all_to_all(copies, axis, 0, 0, axis_index_groups=groups)  12.3 us
    all_to_all x1, blocking collectives, to_all(): return lax.all_to_all(copies, axis, 0, 0, axis_index_groups=groups)  10.8 us
    ppermute x8, waiting for transfers between devices, send(): return lax.ppermute(array, ('row', 'col'), pairs)  6.04 us
  transfers between devices with their start and end apart: 11, of which 6 were waited for; matrix products, arithmetic and copies ran while one was open for 1% of the time, Pallas kernels for 20%

profile of v4, /device:TPU:1, one launch (start us, length us, event | category | flops | bytes accessed | tf_op | source)
XLA Modules:
  0.0 115.7 jit_solution(3820724014823919610)
XLA Ops:
  6.5 0.9 copy.6
  7.5 0.8 broadcast_in_dim.9
  8.3 10.9 %all-to-all-start = ((f32[8,128,128]{2,1,0:T(8,128)}), f32[8,128,128]{2,1,0:T(8,128)S(1)}, u32[]{:S(2)}, u32[]{:S(2)}) async-start(f32[8,128,128]{2,1,0:T(8,128)} %broadcast_in_dim.9), calls=%async_computation | async-start | bytes 1048576 | tf_op jit(solution)/shard_map/all_to_all | solution.py:236
  19.2 4.5 %collective-permute-start = (f32[128,256]{1,0:T(8,128)S(1)}, f32[128,256]{1,0:T(8,128)S(1)}, u32[]{:S(2)}, u32[]{:S(2)}) collective-permute-start(f32[128,256]{1,0:T(8,128)S(1)} %bitcast.28), channel_id=1, source_target_pairs={{0,384},{1,385},{2,386},{3,387},{4,388},{5,389},{6,390},{7,391},{8... | collective-permute-start | bytes 393224 | tf_op jit(solution)/shard_map/ppermute | solution.py:209
  23.7 1.3 %collective-permute-start.1 = (f32[128,256]{1,0:T(8,128)S(1)}, f32[128,256]{1,0:T(8,128)S(1)}, u32[]{:S(2)}, u32[]{:S(2)}) collective-permute-start(f32[128,256]{1,0:T(8,128)S(1)} %bitcast.29), channel_id=1, source_target_pairs={{0,256},{1,257},{2,258},{3,259},{4,260},{5,261},{6,262},{7,263},{8... | collective-permute-start | bytes 393224 | tf_op jit(solution)/shard_map/ppermute | solution.py:209
  25.0 1.3 %collective-permute-start.2 = (f32[128,256]{1,0:T(8,128)S(1)}, f32[128,256]{1,0:T(8,128)S(1)}, u32[]{:S(2)}, u32[]{:S(2)}) collective-permute-start(f32[128,256]{1,0:T(8,128)S(1)} %bitcast.30), channel_id=1, source_target_pairs={{0,128},{1,129},{2,130},{3,131},{4,132},{5,133},{6,134},{7,135},{8... | collective-permute-start | bytes 393224 | tf_op jit(solution)/shard_map/ppermute | solution.py:209
  26.4 0.0 collective-permute-done
  26.4 0.5 collective-permute-done.1
  26.9 2.7 %collective-permute-done.2 = f32[128,256]{1,0:T(8,128)S(1)} collective-permute-done((f32[128,256]{1,0:T(8,128)S(1)}, f32[128,256]{1,0:T(8,128)S(1)}, u32[]{:S(2)}, u32[]{:S(2)}) %collective-permute-start.2) | collective-permute-done | bytes 131104 | tf_op jit(solution)/shard_map/ppermute | solution.py:209
  29.6 0.7 select_select_fusion
  30.3 6.8 %all-to-all-done = f32[8,128,128]{2,1,0:T(8,128)S(1)} async-done(((f32[8,128,128]{2,1,0:T(8,128)}), f32[8,128,128]{2,1,0:T(8,128)S(1)}, u32[]{:S(2)}, u32[]{:S(2)}) %all-to-all-start) | async-done | bytes 524320 | tf_op jit(solution)/shard_map/all_to_all | solution.py:236
  37.2 4.4 %collective-permute-start.3 = (f32[64,128]{1,0:T(8,128)S(1)}, f32[64,128]{1,0:T(8,128)S(1)}, u32[]{:S(2)}, u32[]{:S(2)}) collective-permute-start(f32[64,128]{1,0:T(8,128)S(1)} %get-tuple-element.19), channel_id=1, source_target_pairs={{0,384},{1,385},{2,386},{3,387},{4,388},{5,389},{6,390},{7,391},{8... | collective-permute-start | bytes 98312 | tf_op jit(solution)/shard_map/ppermute | solution.py:209
  41.6 1.3 %collective-permute-start.4 = (f32[64,128]{1,0:T(8,128)S(1)}, f32[64,128]{1,0:T(8,128)S(1)}, u32[]{:S(2)}, u32[]{:S(2)}) collective-permute-start(f32[64,128]{1,0:T(8,128)S(1)} %get-tuple-element.18), channel_id=1, source_target_pairs={{0,256},{1,257},{2,258},{3,259},{4,260},{5,261},{6,262},{7,263},{8... | collective-permute-start | bytes 98312 | tf_op jit(solution)/shard_map/ppermute | solution.py:209
  42.9 1.3 %collective-permute-start.5 = (f32[64,128]{1,0:T(8,128)S(1)}, f32[64,128]{1,0:T(8,128)S(1)}, u32[]{:S(2)}, u32[]{:S(2)}) collective-permute-start(f32[64,128]{1,0:T(8,128)S(1)} %get-tuple-element.17), channel_id=1, source_target_pairs={{0,128},{1,129},{2,130},{3,131},{4,132},{5,133},{6,134},{7,135},{8... | collective-permute-start | bytes 98312 | tf_op jit(solution)/shard_map/ppermute | solution.py:209
  44.2 0.0 collective-permute-done.3
  44.2 1.0 collective-permute-done.5
  45.2 0.7 broadcast_in_dim.10
  45.9 6.8 %all-to-all-start.1 = ((f32[8,64,128]{2,1,0:T(8,128)}), f32[8,64,128]{2,1,0:T(8,128)S(1)}, u32[]{:S(2)}, u32[]{:S(2)}) async-start(f32[8,64,128]{2,1,0:T(8,128)} %broadcast_in_dim.10), calls=%async_computation.1 | async-start | bytes 524288 | tf_op jit(solution)/shard_map/all_to_all | solution.py:236
  52.8 0.0 all-gather.3.cloned.1.call-start
  52.8 0.7 all-gather.3.cloned.1.call-update
  53.5 3.5 %collective-permute-start.6 = (f32[3,128,128]{2,1,0:T(8,128)S(1)}, f32[3,128,128]{2,1,0:T(8,128)S(1)}, u32[]{:S(2)}, u32[]{:S(2)}) collective-permute-start(f32[3,128,128]{2,1,0:T(8,128)S(1)} %slice.33.near_row), channel_id=1, source_target_pairs={{0,1},{1,0},{2,3},{3,2},{4,5},{5,4},{6,7},{7,6},{8,9},{9,8},{10,11... | collective-permute-start | bytes 589832 | tf_op jit(solution)/shard_map/ppermute | solution.py:209
  57.0 5.5 %all-to-all-done.1 = f32[8,64,128]{2,1,0:T(8,128)S(1)} async-done(((f32[8,64,128]{2,1,0:T(8,128)}), f32[8,64,128]{2,1,0:T(8,128)S(1)}, u32[]{:S(2)}, u32[]{:S(2)}) %all-to-all-start.1) | async-done | bytes 262176 | tf_op jit(solution)/shard_map/all_to_all | solution.py:236
  62.6 0.1 broadcast_in_dim.11
  62.7 10.8 %all_to_all.15.near = f32[4,6,64,128]{3,2,1,0:T(8,128)S(1)} all-to-all(f32[4,6,64,128]{3,2,1,0:T(8,128)S(1)} %broadcast_in_dim.11), channel_id=1, replica_groups={{0,128,256,384},{16,144,272,400},{32,160,288,416},{48,176,304,432},{64,..., dimensions={0} | all-to-all | bytes 1572864 | tf_op jit(solution)/shard_map/all_to_all | solution.py:236
  73.4 7.0 %collective-permute-start.7 = (f32[4,6,64,128]{3,2,1,0:T(8,128)S(1)}, f32[4,6,64,128]{3,2,1,0:T(8,128)S(1)}, u32[]{:S(2)}, u32[]{:S(2)}) collective-permute-start(f32[4,6,64,128]{3,2,1,0:T(8,128)S(1)} %all_to_all.15.near), channel_id=1, source_target_pairs={{0,1},{1,0},{2,3},{3,2},{4,5},{5,4},{6,7},{7,6},{8,9},{9,8},{10,11... | collective-permute-start | bytes 2359304 | tf_op jit(solution)/shard_map/ppermute | solution.py:209
  80.4 0.1 pad_add_fusion.place
  80.5 1.8 %collective-permute-done.7.far = f32[4,6,64,128]{3,2,1,0:T(8,128)S(1)} collective-permute-done((f32[4,6,64,128]{3,2,1,0:T(8,128)S(1)}, f32[4,6,64,128]{3,2,1,0:T(8,128)S(1)}, u32[]{:S(2)}, u32[]{:S(2)}) %collective-permute-start.7) | collective-permute-done | bytes 786464 | tf_op jit(solution)/shard_map/ppermute | solution.py:209
  82.3 23.4 %shard_map.17 = (f32[128,768]{1,0:T(8,128)S(1)}, f32[128,768]{1,0:T(8,128)S(1)}) custom-call(s32[3]{0:T(128)S(1)} %pad_add_fusion.place, f32[4,6,64,128]{3,2,1,0:T(8,128)S(1)} %all_to_all.15.near, f32[4,6,64,128]{3,2,1,0:T(8,128)S(1)} %collective-permute-done.7.far, f32[3,128,128]{2,1,0:T(8,128)S(1)} %slice.33.near_row, ...), custom_call_target="tpu_custom_call" | custom-call | flops 1 | bytes 1 | tf_op jit(solution)/shard_map/pallas_call | solution.py:269
  105.7 0.0 all-gather.3.cloned.1.call-done
  105.8 1.2 %copy-done = f32[1024,256]{1,0:T(8,128)S(1)} copy-done((f32[1024,256]{1,0:T(8,128)S(1)}, f32[1024,256]{1,0:T(8,128)}, u32[]{:S(2)}) %copy-start) | copy-done | bytes 1048600
  107.0 1.1 shard_map.18
  108.1 0.7 reshape.11
  (12 shorter events, 0.1 us)
Async XLA Ops:
  8.3 28.8 %all-to-all-start = ((f32[8,128,128]{2,1,0:T(8,128)}), f32[8,128,128]{2,1,0:T(8,128)S(1)}, u32[]{:S(2)}, u32[]{:S(2)}) async-start(f32[8,128,128]{2,1,0:T(8,128)} %broadcast_in_dim.9), calls=%async_computation | async-start | bytes 1048576 | tf_op jit(solution)/shard_map/all_to_all | solution.py:236
  19.2 10.5 %copy-start.1 = (f32[1,128,2,128]{3,2,1,0:T(2,128)S(1)}, f32[1,128,2,128]{3,2,1,0:T(2,128)}, u32[]{:S(2)}) copy-start(f32[1,128,2,128]{3,2,1,0:T(2,128)} %param.1) | copy-start | bytes 393220
  19.2 7.2 %collective-permute-start = (f32[128,256]{1,0:T(8,128)S(1)}, f32[128,256]{1,0:T(8,128)S(1)}, u32[]{:S(2)}, u32[]{:S(2)}) collective-permute-start(f32[128,256]{1,0:T(8,128)S(1)} %bitcast.28), channel_id=1, source_target_pairs={{0,384},{1,385},{2,386},{3,387},{4,388},{5,389},{6,390},{7,391},{8... | collective-permute-start | bytes 393224 | tf_op jit(solution)/shard_map/ppermute | solution.py:209
  23.7 3.2 %collective-permute-start.1 = (f32[128,256]{1,0:T(8,128)S(1)}, f32[128,256]{1,0:T(8,128)S(1)}, u32[]{:S(2)}, u32[]{:S(2)}) collective-permute-start(f32[128,256]{1,0:T(8,128)S(1)} %bitcast.29), channel_id=1, source_target_pairs={{0,256},{1,257},{2,258},{3,259},{4,260},{5,261},{6,262},{7,263},{8... | collective-permute-start | bytes 393224 | tf_op jit(solution)/shard_map/ppermute | solution.py:209
  25.0 4.6 %collective-permute-start.2 = (f32[128,256]{1,0:T(8,128)S(1)}, f32[128,256]{1,0:T(8,128)S(1)}, u32[]{:S(2)}, u32[]{:S(2)}) collective-permute-start(f32[128,256]{1,0:T(8,128)S(1)} %bitcast.30), channel_id=1, source_target_pairs={{0,128},{1,129},{2,130},{3,131},{4,132},{5,133},{6,134},{7,135},{8... | collective-permute-start | bytes 393224 | tf_op jit(solution)/shard_map/ppermute | solution.py:209
  37.2 7.0 %collective-permute-start.3 = (f32[64,128]{1,0:T(8,128)S(1)}, f32[64,128]{1,0:T(8,128)S(1)}, u32[]{:S(2)}, u32[]{:S(2)}) collective-permute-start(f32[64,128]{1,0:T(8,128)S(1)} %get-tuple-element.19), channel_id=1, source_target_pairs={{0,384},{1,385},{2,386},{3,387},{4,388},{5,389},{6,390},{7,391},{8... | collective-permute-start | bytes 98312 | tf_op jit(solution)/shard_map/ppermute | solution.py:209
  41.6 2.6 %collective-permute-start.4 = (f32[64,128]{1,0:T(8,128)S(1)}, f32[64,128]{1,0:T(8,128)S(1)}, u32[]{:S(2)}, u32[]{:S(2)}) collective-permute-start(f32[64,128]{1,0:T(8,128)S(1)} %get-tuple-element.18), channel_id=1, source_target_pairs={{0,256},{1,257},{2,258},{3,259},{4,260},{5,261},{6,262},{7,263},{8... | collective-permute-start | bytes 98312 | tf_op jit(solution)/shard_map/ppermute | solution.py:209
  42.9 2.3 %collective-permute-start.5 = (f32[64,128]{1,0:T(8,128)S(1)}, f32[64,128]{1,0:T(8,128)S(1)}, u32[]{:S(2)}, u32[]{:S(2)}) collective-permute-start(f32[64,128]{1,0:T(8,128)S(1)} %get-tuple-element.17), channel_id=1, source_target_pairs={{0,128},{1,129},{2,130},{3,131},{4,132},{5,133},{6,134},{7,135},{8... | collective-permute-start | bytes 98312 | tf_op jit(solution)/shard_map/ppermute | solution.py:209
  45.9 16.6 %all-to-all-start.1 = ((f32[8,64,128]{2,1,0:T(8,128)}), f32[8,64,128]{2,1,0:T(8,128)S(1)}, u32[]{:S(2)}, u32[]{:S(2)}) async-start(f32[8,64,128]{2,1,0:T(8,128)} %broadcast_in_dim.10), calls=%async_computation.1 | async-start | bytes 524288 | tf_op jit(solution)/shard_map/all_to_all | solution.py:236
  52.8 53.0 %all-gather.3.cloned.1.call-start = ((), (), s32[]{:S(2)}) async-start(), calls=%async_computation.3 | async-start | bytes 1179648 | tf_op jit(solution)/shard_map/all_gather | solution.py:249
  53.5 9.1 %collective-permute-start.6 = (f32[3,128,128]{2,1,0:T(8,128)S(1)}, f32[3,128,128]{2,1,0:T(8,128)S(1)}, u32[]{:S(2)}, u32[]{:S(2)}) collective-permute-start(f32[3,128,128]{2,1,0:T(8,128)S(1)} %slice.33.near_row), channel_id=1, source_target_pairs={{0,1},{1,0},{2,3},{3,2},{4,5},{5,4},{6,7},{7,6},{8,9},{9,8},{10,11... | collective-permute-start | bytes 589832 | tf_op jit(solution)/shard_map/ppermute | solution.py:209
  73.4 8.9 %collective-permute-start.7 = (f32[4,6,64,128]{3,2,1,0:T(8,128)S(1)}, f32[4,6,64,128]{3,2,1,0:T(8,128)S(1)}, u32[]{:S(2)}, u32[]{:S(2)}) collective-permute-start(f32[4,6,64,128]{3,2,1,0:T(8,128)S(1)} %all_to_all.15.near), channel_id=1, source_target_pairs={{0,1},{1,0},{2,3},{3,2},{4,5},{5,4},{6,7},{7,6},{8,9},{9,8},{10,11... | collective-permute-start | bytes 2359304 | tf_op jit(solution)/shard_map/ppermute | solution.py:209
  105.8 1.2 %copy-start = (f32[1024,256]{1,0:T(8,128)S(1)}, f32[1024,256]{1,0:T(8,128)}, u32[]{:S(2)}) copy-start(f32[1024,256]{1,0:T(8,128)} %all-gather.3.cloned.1.call-done) | copy-start | bytes 3145732
Sparse Core Ops, SparseCore 0:
  55.7 33.1 all-gather.2

commit v5 on v4

--- a/solution.py
+++ b/solution.py
@@ -7,8 +7,9 @@
 
 TILE = 128
 NB = 6
-GROUP = 32
-WINDOW = 16
+GROUP = 64
+LAG = 1
+WINDOW = 8
 XS, YS, ZS = 4, 8, 8
 SENT = NB // 2 + 1
 ZSRC = NB // 2
@@ -29,21 +30,23 @@
 
 
 def eliminate(rows, offset):
-    count, width = rows.shape
+    count = rows.shape[0]
     groups = count // 8
-
-    def wide(value):
-        return jnp.concatenate([value] * (width // TILE), axis=1)
-
     part = [rows[8 * g : 8 * g + 8] for g in range(groups)]
     sublane = lax.broadcasted_iota(jnp.int32, (8, TILE), 0)
+    lane = lax.broadcasted_iota(jnp.int32, (8, TILE), 1)
     scale = [None] * groups
-    for start in range(0, count, WINDOW):
-        column = {}
+    column = {}
+
+    def take(start):
         for j in range(start, start + WINDOW):
             for g in range(j // 8, groups):
-                lane = offset + j
-                column[g, j] = jnp.broadcast_to(part[g][:, lane : lane + 1], (8, TILE))
+                at = offset + j
+                column[g, j] = jnp.broadcast_to(part[g][:, at : at + 1], (8, TILE))
+
+    take(0)
+    taken_to = WINDOW
+    for start in range(0, count, WINDOW):
         for k in range(start, start + WINDOW, 2):
             gk, sk = divmod(k, 8)
             first = spread(column[gk, k][sk : sk + 1])
@@ -54,50 +57,48 @@
             factor = {}
             for g in range(gk, groups):
                 a, b = column[g, k], column[g, k + 1]
-                factor[g] = [a * second - b * cross, b * first - a * cross]
-            for j in range(k + 2, min(k + 4, start + WINDOW)):
-                gj, sj = divmod(j, 8)
-                across = [spread(column[gj, k + i][sj : sj + 1]) for i in range(2)]
-                for g in range(gj, groups):
-                    taken = factor[g][0] * across[0] + factor[g][1] * across[1]
-                    column[g, j] = column[g, j] - taken * inverse
-            for g in range(gk, groups):
-                factor[g] = [value * inverse for value in factor[g]]
-            for j in range(k + 4, start + WINDOW):
+                factor[g] = [(a * second - b * cross) * inverse, (b * first - a * cross) * inverse]
+            for j in range(k + 2, taken_to):
                 gj, sj = divmod(j, 8)
                 across = [spread(column[gj, k + i][sj : sj + 1]) for i in range(2)]
                 for g in range(gj, groups):
                     column[g, j] = column[g, j] - (factor[g][0] * across[0] + factor[g][1] * across[1])
-            factor[gk] = [jnp.where(sublane > sk + 1, value, 0.0) for value in factor[gk]]
-            pivot_rows = [spread(part[gk][sk + i : sk + i + 1]) for i in range(2)]
             reciprocal = pl.reciprocal(first)
             roots = [lax.rsqrt(first), lax.rsqrt(determinant * reciprocal)]
             own = jnp.where(sublane == sk, roots[0], jnp.where(sublane == sk + 1, roots[1], 1.0))
             scale[gk] = own if scale[gk] is None else scale[gk] * own
-            inside = jnp.where(sublane == sk + 1, cross * reciprocal, 0.0)
-            for g in range(gk, groups):
-                taken = wide(factor[g][0]) * pivot_rows[0] + wide(factor[g][1]) * pivot_rows[1]
-                if g == gk:
-                    taken = taken + wide(inside) * pivot_rows[0]
-                part[g] = part[g] - taken
-    return jnp.concatenate([part[g] * wide(scale[g]) for g in range(groups)], axis=0)
+            pair = (lane >= offset + k) & (lane < offset + k + 2)
+            diagonal = lane - (offset + k) == sublane - sk
+            part[gk] = jnp.where(pair & (sublane >= sk), jnp.where(diagonal & (sublane < sk + 2), 1.0, 0.0), part[gk])
+            pivot_rows = [spread(part[gk][sk + i : sk + i + 1]) for i in range(2)]
+            below = [jnp.where(sublane > sk + 1, value, 0.0) for value in factor[gk]]
+            below[0] = below[0] + jnp.where(sublane == sk + 1, cross * reciprocal, 0.0)
+            part[gk] = part[gk] - (below[0] * pivot_rows[0] + below[1] * pivot_rows[1])
+            for g in range(gk + 1, groups):
+                taken = factor[g][0] * pivot_rows[0] + factor[g][1] * pivot_rows[1]
+                part[g] = jnp.where(pair, 0.0, part[g]) - taken
+            if k + 2 + 2 * LAG == start + WINDOW and taken_to < count:
+                take(taken_to)
+                taken_to += WINDOW
+    return jnp.concatenate([part[g] * scale[g] for g in range(groups)], axis=0)
 
 
 def factor_tile(tile, beside):
     row = lax.broadcasted_iota(jnp.int32, (TILE, TILE), 0)
     lane = lax.broadcasted_iota(jnp.int32, (TILE, TILE), 1)
-    both = jnp.concatenate([tile, jnp.where(row == lane, 1.0, 0.0)], axis=1)
-    upper = None
+    done = None
     for start in range(0, TILE, GROUP):
-        rows = both[start : start + GROUP]
-        if upper is not None:
-            rows = rows - dot(upper.T[start : start + GROUP], upper)
+        rows = tile[start : start + GROUP]
+        if done is not None:
+            mask = (lane[:start] <= row[:start]) | (lane[:start] >= start)
+            rows = jnp.where(lane[:GROUP] >= start, rows, 0.0)
+            rows = rows - dot(done.T[start : start + GROUP], jnp.where(mask, done, 0.0))
         rows = eliminate(rows, start)
-        upper = rows if upper is None else jnp.concatenate([upper, rows], axis=0)
+        done = rows if done is None else jnp.concatenate([done, rows], axis=0)
         slot, slots = start // GROUP, TILE // GROUP
         for task in beside[slot * len(beside) // slots : (slot + 1) * len(beside) // slots]:
             task()
-    return upper[:, TILE:]
+    return jnp.where(lane <= row, done, 0.0)
 
 
 def dot_nt(a, b):

time: 116 us -> 113 us (0.974)
  Pallas kernels: 24.6 us -> 21.4 us
    pallas_call x1, Pallas kernels: 23.4 us -> 20.3 us  [per_device(): pl.pallas_call(factor_kernel, out_shape=[jax.ShapeDtypeStruct((TILE, orde...]
  transfers between devices with their start and end apart: 11 -> 11, of which waited for: 6 -> 6; matrix products, arithmetic and copies ran while one was open for 1% -> 1% of each run, Pallas kernels for 20% -> 18%
where the time goes in v5:
time: 113 us
  starting transfers between devices  42.3 us (37%)
  Pallas kernels  21.4 us (19%)
  waiting for transfers between devices  19 us (17%)
  between operations  13.7 us (12%)
  blocking collectives  10.8 us (10%)
  local copies, waits for them, and re-layouts  4.55 us (4%)
    ppermute x8, starting transfers between devices, send(): return lax.ppermute(array, ('row', 'col'), pairs)  24.6 us
    pallas_call x1, Pallas kernels, per_device(): pl.pallas_call(factor_kernel, out_shape=[jax.ShapeDtypeStruct((TILE, orde...  20.3 us
    all_to_all x2, starting transfers between devices, to_all(): return lax.all_to_all(copies, axis, 0, 0, axis_index_groups=groups)  17.7 us
    all_to_all x2, waiting for transfers between devices, to_all(): return lax.all_to_all(copies, axis, 0, 0, axis_index_groups=groups)  12.3 us
    all_to_all x1, blocking collectives, to_all(): return lax.all_to_all(copies, axis, 0, 0, axis_index_groups=groups)  10.8 us
    ppermute x8, waiting for transfers between devices, send(): return lax.ppermute(array, ('row', 'col'), pairs)  6.04 us
  transfers between devices with their start and end apart: 11, of which 6 were waited for; matrix products, arithmetic and copies ran while one was open for 1% of the time, Pallas kernels for 18%

profile of v5, /device:TPU:1, one launch (start us, length us, event | category | flops | bytes accessed | tf_op | source)
XLA Modules:
  0.0 112.6 jit_solution(8951814250783648368)
XLA Ops:
  6.5 0.9 copy.6
  7.5 0.8 broadcast_in_dim.9
  8.3 10.9 %all-to-all-start = ((f32[8,128,128]{2,1,0:T(8,128)}), f32[8,128,128]{2,1,0:T(8,128)S(1)}, u32[]{:S(2)}, u32[]{:S(2)}) async-start(f32[8,128,128]{2,1,0:T(8,128)} %broadcast_in_dim.9), calls=%async_computation | async-start | bytes 1048576 | tf_op jit(solution)/shard_map/all_to_all | solution.py:237
  19.2 4.5 %collective-permute-start = (f32[128,256]{1,0:T(8,128)S(1)}, f32[128,256]{1,0:T(8,128)S(1)}, u32[]{:S(2)}, u32[]{:S(2)}) collective-permute-start(f32[128,256]{1,0:T(8,128)S(1)} %bitcast.28), channel_id=1, source_target_pairs={{0,384},{1,385},{2,386},{3,387},{4,388},{5,389},{6,390},{7,391},{8... | collective-permute-start | bytes 393224 | tf_op jit(solution)/shard_map/ppermute | solution.py:210
  23.7 1.3 %collective-permute-start.1 = (f32[128,256]{1,0:T(8,128)S(1)}, f32[128,256]{1,0:T(8,128)S(1)}, u32[]{:S(2)}, u32[]{:S(2)}) collective-permute-start(f32[128,256]{1,0:T(8,128)S(1)} %bitcast.29), channel_id=1, source_target_pairs={{0,256},{1,257},{2,258},{3,259},{4,260},{5,261},{6,262},{7,263},{8... | collective-permute-start | bytes 393224 | tf_op jit(solution)/shard_map/ppermute | solution.py:210
  25.0 1.3 %collective-permute-start.2 = (f32[128,256]{1,0:T(8,128)S(1)}, f32[128,256]{1,0:T(8,128)S(1)}, u32[]{:S(2)}, u32[]{:S(2)}) collective-permute-start(f32[128,256]{1,0:T(8,128)S(1)} %bitcast.30), channel_id=1, source_target_pairs={{0,128},{1,129},{2,130},{3,131},{4,132},{5,133},{6,134},{7,135},{8... | collective-permute-start | bytes 393224 | tf_op jit(solution)/shard_map/ppermute | solution.py:210
  26.4 0.0 collective-permute-done
  26.4 0.5 collective-permute-done.1
  26.9 2.7 %collective-permute-done.2 = f32[128,256]{1,0:T(8,128)S(1)} collective-permute-done((f32[128,256]{1,0:T(8,128)S(1)}, f32[128,256]{1,0:T(8,128)S(1)}, u32[]{:S(2)}, u32[]{:S(2)}) %collective-permute-start.2) | collective-permute-done | bytes 131104 | tf_op jit(solution)/shard_map/ppermute | solution.py:210
  29.6 0.7 select_select_fusion
  30.3 6.8 %all-to-all-done = f32[8,128,128]{2,1,0:T(8,128)S(1)} async-done(((f32[8,128,128]{2,1,0:T(8,128)}), f32[8,128,128]{2,1,0:T(8,128)S(1)}, u32[]{:S(2)}, u32[]{:S(2)}) %all-to-all-start) | async-done | bytes 524320 | tf_op jit(solution)/shard_map/all_to_all | solution.py:237
  37.2 4.4 %collective-permute-start.3 = (f32[64,128]{1,0:T(8,128)S(1)}, f32[64,128]{1,0:T(8,128)S(1)}, u32[]{:S(2)}, u32[]{:S(2)}) collective-permute-start(f32[64,128]{1,0:T(8,128)S(1)} %get-tuple-element.19), channel_id=1, source_target_pairs={{0,384},{1,385},{2,386},{3,387},{4,388},{5,389},{6,390},{7,391},{8... | collective-permute-start | bytes 98312 | tf_op jit(solution)/shard_map/ppermute | solution.py:210
  41.6 1.3 %collective-permute-start.4 = (f32[64,128]{1,0:T(8,128)S(1)}, f32[64,128]{1,0:T(8,128)S(1)}, u32[]{:S(2)}, u32[]{:S(2)}) collective-permute-start(f32[64,128]{1,0:T(8,128)S(1)} %get-tuple-element.18), channel_id=1, source_target_pairs={{0,256},{1,257},{2,258},{3,259},{4,260},{5,261},{6,262},{7,263},{8... | collective-permute-start | bytes 98312 | tf_op jit(solution)/shard_map/ppermute | solution.py:210
  42.9 1.3 %collective-permute-start.5 = (f32[64,128]{1,0:T(8,128)S(1)}, f32[64,128]{1,0:T(8,128)S(1)}, u32[]{:S(2)}, u32[]{:S(2)}) collective-permute-start(f32[64,128]{1,0:T(8,128)S(1)} %get-tuple-element.17), channel_id=1, source_target_pairs={{0,128},{1,129},{2,130},{3,131},{4,132},{5,133},{6,134},{7,135},{8... | collective-permute-start | bytes 98312 | tf_op jit(solution)/shard_map/ppermute | solution.py:210
  44.2 1.0 collective-permute-done.5
  45.2 0.7 broadcast_in_dim.10
  45.9 6.8 %all-to-all-start.1 = ((f32[8,64,128]{2,1,0:T(8,128)}), f32[8,64,128]{2,1,0:T(8,128)S(1)}, u32[]{:S(2)}, u32[]{:S(2)}) async-start(f32[8,64,128]{2,1,0:T(8,128)} %broadcast_in_dim.10), calls=%async_computation.1 | async-start | bytes 524288 | tf_op jit(solution)/shard_map/all_to_all | solution.py:237
  52.8 0.0 all-gather.3.cloned.1.call-start
  52.8 0.7 all-gather.3.cloned.1.call-update
  53.5 3.5 %collective-permute-start.6 = (f32[3,128,128]{2,1,0:T(8,128)S(1)}, f32[3,128,128]{2,1,0:T(8,128)S(1)}, u32[]{:S(2)}, u32[]{:S(2)}) collective-permute-start(f32[3,128,128]{2,1,0:T(8,128)S(1)} %slice.33.near_row), channel_id=1, source_target_pairs={{0,1},{1,0},{2,3},{3,2},{4,5},{5,4},{6,7},{7,6},{8,9},{9,8},{10,11... | collective-permute-start | bytes 589832 | tf_op jit(solution)/shard_map/ppermute | solution.py:210
  57.0 5.5 %all-to-all-done.1 = f32[8,64,128]{2,1,0:T(8,128)S(1)} async-done(((f32[8,64,128]{2,1,0:T(8,128)}), f32[8,64,128]{2,1,0:T(8,128)S(1)}, u32[]{:S(2)}, u32[]{:S(2)}) %all-to-all-start.1) | async-done | bytes 262176 | tf_op jit(solution)/shard_map/all_to_all | solution.py:237
  62.6 0.0 collective-permute-done.6.far_row
  62.6 0.1 broadcast_in_dim.11
  62.7 10.8 %all_to_all.15.near = f32[4,6,64,128]{3,2,1,0:T(8,128)S(1)} all-to-all(f32[4,6,64,128]{3,2,1,0:T(8,128)S(1)} %broadcast_in_dim.11), channel_id=1, replica_groups={{0,128,256,384},{16,144,272,400},{32,160,288,416},{48,176,304,432},{64,..., dimensions={0} | all-to-all | bytes 1572864 | tf_op jit(solution)/shard_map/all_to_all | solution.py:237
  73.4 7.0 %collective-permute-start.7 = (f32[4,6,64,128]{3,2,1,0:T(8,128)S(1)}, f32[4,6,64,128]{3,2,1,0:T(8,128)S(1)}, u32[]{:S(2)}, u32[]{:S(2)}) collective-permute-start(f32[4,6,64,128]{3,2,1,0:T(8,128)S(1)} %all_to_all.15.near), channel_id=1, source_target_pairs={{0,1},{1,0},{2,3},{3,2},{4,5},{5,4},{6,7},{7,6},{8,9},{9,8},{10,11... | collective-permute-start | bytes 2359304 | tf_op jit(solution)/shard_map/ppermute | solution.py:210
  80.4 0.1 pad_add_fusion.place
  80.5 1.8 %collective-permute-done.7.far = f32[4,6,64,128]{3,2,1,0:T(8,128)S(1)} collective-permute-done((f32[4,6,64,128]{3,2,1,0:T(8,128)S(1)}, f32[4,6,64,128]{3,2,1,0:T(8,128)S(1)}, u32[]{:S(2)}, u32[]{:S(2)}) %collective-permute-start.7) | collective-permute-done | bytes 786464 | tf_op jit(solution)/shard_map/ppermute | solution.py:210
  82.3 20.3 %shard_map.17 = (f32[128,768]{1,0:T(8,128)S(1)}, f32[128,768]{1,0:T(8,128)S(1)}) custom-call(s32[3]{0:T(128)S(1)} %pad_add_fusion.place, f32[4,6,64,128]{3,2,1,0:T(8,128)S(1)} %all_to_all.15.near, f32[4,6,64,128]{3,2,1,0:T(8,128)S(1)} %collective-permute-done.7.far, f32[3,128,128]{2,1,0:T(8,128)S(1)} %slice.33.near_row, ...), custom_call_target="tpu_custom_call" | custom-call | flops 1 | bytes 1 | tf_op jit(solution)/shard_map/pallas_call | solution.py:270
  102.6 0.0 all-gather.3.cloned.1.call-done
  102.6 1.2 %copy-done = f32[1024,256]{1,0:T(8,128)S(1)} copy-done((f32[1024,256]{1,0:T(8,128)S(1)}, f32[1024,256]{1,0:T(8,128)}, u32[]{:S(2)}) %copy-start) | copy-done | bytes 1048600
  103.8 1.1 %shard_map.18 = f32[128,256]{1,0:T(8,128)S(1)} custom-call(s32[3]{0:T(128)S(1)} %pad_add_fusion.place, f32[128,256]{1,0:T(8,128)S(1)} %bitcast.31, f32[8,128,256]{2,1,0:T(8,128)S(1)} %bitcast.26, f32[128,768]{1,0:T(8,128)S(1)} %get-tuple-element.15.panel, f32[128,768]{1,0:T(8,128)S(1)} %get-tuple-element.16.weights), custom_call_target="tpu_custom_call" | custom-call | tf_op jit(solution)/shard_map/pallas_call | solution.py:279
  105.0 0.7 reshape.11
  (12 shorter events, 0.1 us)
Async XLA Ops:
  8.3 28.8 %all-to-all-start = ((f32[8,128,128]{2,1,0:T(8,128)}), f32[8,128,128]{2,1,0:T(8,128)S(1)}, u32[]{:S(2)}, u32[]{:S(2)}) async-start(f32[8,128,128]{2,1,0:T(8,128)} %broadcast_in_dim.9), calls=%async_computation | async-start | bytes 1048576 | tf_op jit(solution)/shard_map/all_to_all | solution.py:237
  19.2 10.5 %copy-start.1 = (f32[1,128,2,128]{3,2,1,0:T(2,128)S(1)}, f32[1,128,2,128]{3,2,1,0:T(2,128)}, u32[]{:S(2)}) copy-start(f32[1,128,2,128]{3,2,1,0:T(2,128)} %param.1) | copy-start | bytes 393220
  19.2 7.2 %collective-permute-start = (f32[128,256]{1,0:T(8,128)S(1)}, f32[128,256]{1,0:T(8,128)S(1)}, u32[]{:S(2)}, u32[]{:S(2)}) collective-permute-start(f32[128,256]{1,0:T(8,128)S(1)} %bitcast.28), channel_id=1, source_target_pairs={{0,384},{1,385},{2,386},{3,387},{4,388},{5,389},{6,390},{7,391},{8... | collective-permute-start | bytes 393224 | tf_op jit(solution)/shard_map/ppermute | solution.py:210
  23.7 3.2 %collective-permute-start.1 = (f32[128,256]{1,0:T(8,128)S(1)}, f32[128,256]{1,0:T(8,128)S(1)}, u32[]{:S(2)}, u32[]{:S(2)}) collective-permute-start(f32[128,256]{1,0:T(8,128)S(1)} %bitcast.29), channel_id=1, source_target_pairs={{0,256},{1,257},{2,258},{3,259},{4,260},{5,261},{6,262},{7,263},{8... | collective-permute-start | bytes 393224 | tf_op jit(solution)/shard_map/ppermute | solution.py:210
  25.0 4.6 %collective-permute-start.2 = (f32[128,256]{1,0:T(8,128)S(1)}, f32[128,256]{1,0:T(8,128)S(1)}, u32[]{:S(2)}, u32[]{:S(2)}) collective-permute-start(f32[128,256]{1,0:T(8,128)S(1)} %bitcast.30), channel_id=1, source_target_pairs={{0,128},{1,129},{2,130},{3,131},{4,132},{5,133},{6,134},{7,135},{8... | collective-permute-start | bytes 393224 | tf_op jit(solution)/shard_map/ppermute | solution.py:210
  37.2 7.0 %collective-permute-start.3 = (f32[64,128]{1,0:T(8,128)S(1)}, f32[64,128]{1,0:T(8,128)S(1)}, u32[]{:S(2)}, u32[]{:S(2)}) collective-permute-start(f32[64,128]{1,0:T(8,128)S(1)} %get-tuple-element.19), channel_id=1, source_target_pairs={{0,384},{1,385},{2,386},{3,387},{4,388},{5,389},{6,390},{7,391},{8... | collective-permute-start | bytes 98312 | tf_op jit(solution)/shard_map/ppermute | solution.py:210
  41.6 2.6 %collective-permute-start.4 = (f32[64,128]{1,0:T(8,128)S(1)}, f32[64,128]{1,0:T(8,128)S(1)}, u32[]{:S(2)}, u32[]{:S(2)}) collective-permute-start(f32[64,128]{1,0:T(8,128)S(1)} %get-tuple-element.18), channel_id=1, source_target_pairs={{0,256},{1,257},{2,258},{3,259},{4,260},{5,261},{6,262},{7,263},{8... | collective-permute-start | bytes 98312 | tf_op jit(solution)/shard_map/ppermute | solution.py:210
  42.9 2.3 %collective-permute-start.5 = (f32[64,128]{1,0:T(8,128)S(1)}, f32[64,128]{1,0:T(8,128)S(1)}, u32[]{:S(2)}, u32[]{:S(2)}) collective-permute-start(f32[64,128]{1,0:T(8,128)S(1)} %get-tuple-element.17), channel_id=1, source_target_pairs={{0,128},{1,129},{2,130},{3,131},{4,132},{5,133},{6,134},{7,135},{8... | collective-permute-start | bytes 98312 | tf_op jit(solution)/shard_map/ppermute | solution.py:210
  45.9 16.6 %all-to-all-start.1 = ((f32[8,64,128]{2,1,0:T(8,128)}), f32[8,64,128]{2,1,0:T(8,128)S(1)}, u32[]{:S(2)}, u32[]{:S(2)}) async-start(f32[8,64,128]{2,1,0:T(8,128)} %broadcast_in_dim.10), calls=%async_computation.1 | async-start | bytes 524288 | tf_op jit(solution)/shard_map/all_to_all | solution.py:237
  52.8 49.8 %all-gather.3.cloned.1.call-start = ((), (), s32[]{:S(2)}) async-start(), calls=%async_computation.3 | async-start | bytes 1179648 | tf_op jit(solution)/shard_map/all_gather | solution.py:250
  53.5 9.1 %collective-permute-start.6 = (f32[3,128,128]{2,1,0:T(8,128)S(1)}, f32[3,128,128]{2,1,0:T(8,128)S(1)}, u32[]{:S(2)}, u32[]{:S(2)}) collective-permute-start(f32[3,128,128]{2,1,0:T(8,128)S(1)} %slice.33.near_row), channel_id=1, source_target_pairs={{0,1},{1,0},{2,3},{3,2},{4,5},{5,4},{6,7},{7,6},{8,9},{9,8},{10,11... | collective-permute-start | bytes 589832 | tf_op jit(solution)/shard_map/ppermute | solution.py:210
  73.4 8.9 %collective-permute-start.7 = (f32[4,6,64,128]{3,2,1,0:T(8,128)S(1)}, f32[4,6,64,128]{3,2,1,0:T(8,128)S(1)}, u32[]{:S(2)}, u32[]{:S(2)}) collective-permute-start(f32[4,6,64,128]{3,2,1,0:T(8,128)S(1)} %all_to_all.15.near), channel_id=1, source_target_pairs={{0,1},{1,0},{2,3},{3,2},{4,5},{5,4},{6,7},{7,6},{8,9},{9,8},{10,11... | collective-permute-start | bytes 2359304 | tf_op jit(solution)/shard_map/ppermute | solution.py:210
  102.6 1.2 %copy-start = (f32[1024,256]{1,0:T(8,128)S(1)}, f32[1024,256]{1,0:T(8,128)}, u32[]{:S(2)}) copy-start(f32[1024,256]{1,0:T(8,128)} %all-gather.3.cloned.1.call-done) | copy-start | bytes 3145732
Sparse Core Ops, SparseCore 0:
  55.7 33.1 all-gather.2

commit v6 on v5

--- a/solution.py
+++ b/solution.py
@@ -14,6 +14,7 @@
 SENT = NB // 2 + 1
 ZSRC = NB // 2
 VMEM_LIMIT = 48 * 1024 * 1024
+SLAB = 32
 HI = lax.Precision.HIGHEST
 
 
@@ -139,7 +140,7 @@
     own, corner = [], None
     for b in range(NB):
         if b:
-            tile = upper[at(b), at(b)] - dot_t(corner, corner)
+            tile = upper[at(b), at(b)] - dot(corner.T, corner)
         else:
             tile = diagonal_tile(0, 0)
             beside = [place_row(i) for i in range(NB)] + [place_row_strip]
@@ -233,8 +234,10 @@
 
 
 def to_all(array, axis, groups):
-    copies = jnp.broadcast_to(array, (len(groups[0]),) + array.shape)
-    return lax.all_to_all(copies, axis, 0, 0, axis_index_groups=groups)
+    parts = array.reshape((-1, SLAB) + array.shape[-1:])
+    copies = jnp.broadcast_to(parts, (len(groups[0]),) + parts.shape)
+    arrived = lax.all_to_all(copies, axis, 0, 0, axis_index_groups=groups)
+    return arrived.reshape((len(groups[0]),) + array.shape)
 
 
 def per_device(matrix):

time: 113 us -> 113 us (level)
  no operation moved by 1% of the time
where the time goes in v6:
time: 113 us
  starting transfers between devices  42.3 us (37%)
  Pallas kernels  21.4 us (19%)
  waiting for transfers between devices  19 us (17%)
  between operations  13.7 us (12%)
  blocking collectives  10.8 us (10%)
  local copies, waits for them, and re-layouts  4.59 us (4%)
    ppermute x8, starting transfers between devices, send(): return lax.ppermute(array, ('row', 'col'), pairs)  24.6 us
    pallas_call x1, Pallas kernels, per_device(): pl.pallas_call(factor_kernel, out_shape=[jax.ShapeDtypeStruct((TILE, orde...  20.3 us
    all_to_all x2, starting transfers between devices, to_all(): arrived = lax.all_to_all(copies, axis, 0, 0, axis_index_groups=groups)  17.7 us
    all_to_all x2, waiting for transfers between devices, to_all(): arrived = lax.all_to_all(copies, axis, 0, 0, axis_index_groups=groups)  12.3 us
    all_to_all x1, blocking collectives, to_all(): arrived = lax.all_to_all(copies, axis, 0, 0, axis_index_groups=groups)  10.8 us
    ppermute x8, waiting for transfers between devices, send(): return lax.ppermute(array, ('row', 'col'), pairs)  6.04 us
  transfers between devices with their start and end apart: 11, of which 6 were waited for; matrix products, arithmetic and copies ran while one was open for 1% of the time, Pallas kernels for 18%

profile of v6, /device:TPU:1, one launch (start us, length us, event | category | flops | bytes accessed | tf_op | source)
XLA Modules:
  0.0 112.6 jit_solution(12482582820498968720)
XLA Ops:
  6.5 0.9 copy.6
  7.5 0.9 broadcast_in_dim.9
  8.3 10.9 %all-to-all-start = ((f32[8,4,32,128]{3,2,1,0:T(8,128)}), f32[8,4,32,128]{3,2,1,0:T(8,128)S(1)}, u32[]{:S(2)}, u32[]{:S(2)}) async-start(f32[8,4,32,128]{3,2,1,0:T(8,128)} %broadcast_in_dim.9), calls=%async_computation | async-start | bytes 1048576 | tf_op jit(solution)/shard_map/all_to_all | solution.py:239
  19.2 4.5 %collective-permute-start = (f32[128,256]{1,0:T(8,128)S(1)}, f32[128,256]{1,0:T(8,128)S(1)}, u32[]{:S(2)}, u32[]{:S(2)}) collective-permute-start(f32[128,256]{1,0:T(8,128)S(1)} %bitcast.40), channel_id=1, source_target_pairs={{0,384},{1,385},{2,386},{3,387},{4,388},{5,389},{6,390},{7,391},{8... | collective-permute-start | bytes 393224 | tf_op jit(solution)/shard_map/ppermute | solution.py:211
  23.7 1.3 %collective-permute-start.1 = (f32[128,256]{1,0:T(8,128)S(1)}, f32[128,256]{1,0:T(8,128)S(1)}, u32[]{:S(2)}, u32[]{:S(2)}) collective-permute-start(f32[128,256]{1,0:T(8,128)S(1)} %bitcast.41), channel_id=1, source_target_pairs={{0,256},{1,257},{2,258},{3,259},{4,260},{5,261},{6,262},{7,263},{8... | collective-permute-start | bytes 393224 | tf_op jit(solution)/shard_map/ppermute | solution.py:211
  25.0 1.3 %collective-permute-start.2 = (f32[128,256]{1,0:T(8,128)S(1)}, f32[128,256]{1,0:T(8,128)S(1)}, u32[]{:S(2)}, u32[]{:S(2)}) collective-permute-start(f32[128,256]{1,0:T(8,128)S(1)} %bitcast.42), channel_id=1, source_target_pairs={{0,128},{1,129},{2,130},{3,131},{4,132},{5,133},{6,134},{7,135},{8... | collective-permute-start | bytes 393224 | tf_op jit(solution)/shard_map/ppermute | solution.py:211
  26.4 0.0 collective-permute-done
  26.4 0.5 collective-permute-done.1
  27.0 2.7 %collective-permute-done.2 = f32[128,256]{1,0:T(8,128)S(1)} collective-permute-done((f32[128,256]{1,0:T(8,128)S(1)}, f32[128,256]{1,0:T(8,128)S(1)}, u32[]{:S(2)}, u32[]{:S(2)}) %collective-permute-start.2) | collective-permute-done | bytes 131104 | tf_op jit(solution)/shard_map/ppermute | solution.py:211
  29.7 0.7 select_select_fusion
  30.4 6.8 %all-to-all-done = f32[8,4,32,128]{3,2,1,0:T(8,128)S(1)} async-done(((f32[8,4,32,128]{3,2,1,0:T(8,128)}), f32[8,4,32,128]{3,2,1,0:T(8,128)S(1)}, u32[]{:S(2)}, u32[]{:S(2)}) %all-to-all-start) | async-done | bytes 524320 | tf_op jit(solution)/shard_map/all_to_all | solution.py:239
  37.2 4.4 %collective-permute-start.3 = (f32[64,128]{1,0:T(8,128)S(1)}, f32[64,128]{1,0:T(8,128)S(1)}, u32[]{:S(2)}, u32[]{:S(2)}) collective-permute-start(f32[64,128]{1,0:T(8,128)S(1)} %get-tuple-element.19), channel_id=1, source_target_pairs={{0,384},{1,385},{2,386},{3,387},{4,388},{5,389},{6,390},{7,391},{8... | collective-permute-start | bytes 98312 | tf_op jit(solution)/shard_map/ppermute | solution.py:211
  41.6 1.3 %collective-permute-start.4 = (f32[64,128]{1,0:T(8,128)S(1)}, f32[64,128]{1,0:T(8,128)S(1)}, u32[]{:S(2)}, u32[]{:S(2)}) collective-permute-start(f32[64,128]{1,0:T(8,128)S(1)} %get-tuple-element.18), channel_id=1, source_target_pairs={{0,256},{1,257},{2,258},{3,259},{4,260},{5,261},{6,262},{7,263},{8... | collective-permute-start | bytes 98312 | tf_op jit(solution)/shard_map/ppermute | solution.py:211
  42.9 1.3 %collective-permute-start.5 = (f32[64,128]{1,0:T(8,128)S(1)}, f32[64,128]{1,0:T(8,128)S(1)}, u32[]{:S(2)}, u32[]{:S(2)}) collective-permute-start(f32[64,128]{1,0:T(8,128)S(1)} %get-tuple-element.17), channel_id=1, source_target_pairs={{0,128},{1,129},{2,130},{3,131},{4,132},{5,133},{6,134},{7,135},{8... | collective-permute-start | bytes 98312 | tf_op jit(solution)/shard_map/ppermute | solution.py:211
  44.2 0.0 collective-permute-done.3
  44.2 1.0 collective-permute-done.5
  45.2 0.7 broadcast_in_dim.10
  46.0 6.8 %all-to-all-start.1 = ((f32[8,2,32,128]{3,2,1,0:T(8,128)}), f32[8,2,32,128]{3,2,1,0:T(8,128)S(1)}, u32[]{:S(2)}, u32[]{:S(2)}) async-start(f32[8,2,32,128]{3,2,1,0:T(8,128)} %broadcast_in_dim.10), calls=%async_computation.1 | async-start | bytes 524288 | tf_op jit(solution)/shard_map/all_to_all | solution.py:239
  52.8 0.0 all-gather.3.cloned.1.call-start
  52.8 0.7 all-gather.3.cloned.1.call-update
  53.5 3.5 %collective-permute-start.6 = (f32[3,128,128]{2,1,0:T(8,128)S(1)}, f32[3,128,128]{2,1,0:T(8,128)S(1)}, u32[]{:S(2)}, u32[]{:S(2)}) collective-permute-start(f32[3,128,128]{2,1,0:T(8,128)S(1)} %bitcast.36), channel_id=1, source_target_pairs={{0,1},{1,0},{2,3},{3,2},{4,5},{5,4},{6,7},{7,6},{8,9},{9,8},{10,11... | collective-permute-start | bytes 589832 | tf_op jit(solution)/shard_map/ppermute | solution.py:211
  57.1 5.5 %all-to-all-done.1 = f32[8,2,32,128]{3,2,1,0:T(8,128)S(1)} async-done(((f32[8,2,32,128]{3,2,1,0:T(8,128)}), f32[8,2,32,128]{3,2,1,0:T(8,128)S(1)}, u32[]{:S(2)}, u32[]{:S(2)}) %all-to-all-start.1) | async-done | bytes 262176 | tf_op jit(solution)/shard_map/all_to_all | solution.py:239
  62.6 0.1 broadcast_in_dim.11
  62.7 10.8 %all_to_all.15 = f32[4,12,32,128]{3,2,1,0:T(8,128)S(1)} all-to-all(f32[4,12,32,128]{3,2,1,0:T(8,128)S(1)} %broadcast_in_dim.11), channel_id=1, replica_groups={{0,128,256,384},{16,144,272,400},{32,160,288,416},{48,176,304,432},{64,..., dimensions={0} | all-to-all | bytes 1572864 | tf_op jit(solution)/shard_map/all_to_all | solution.py:239
  73.5 7.0 %collective-permute-start.7 = (f32[4,6,64,128]{3,2,1,0:T(8,128)S(1)}, f32[4,6,64,128]{3,2,1,0:T(8,128)S(1)}, u32[]{:S(2)}, u32[]{:S(2)}) collective-permute-start(f32[4,6,64,128]{3,2,1,0:T(8,128)S(1)} %bitcast.32), channel_id=1, source_target_pairs={{0,1},{1,0},{2,3},{3,2},{4,5},{5,4},{6,7},{7,6},{8,9},{9,8},{10,11... | collective-permute-start | bytes 2359304 | tf_op jit(solution)/shard_map/ppermute | solution.py:211
  80.4 0.1 pad_add_fusion.place
  80.5 1.8 %collective-permute-done.7.far = f32[4,6,64,128]{3,2,1,0:T(8,128)S(1)} collective-permute-done((f32[4,6,64,128]{3,2,1,0:T(8,128)S(1)}, f32[4,6,64,128]{3,2,1,0:T(8,128)S(1)}, u32[]{:S(2)}, u32[]{:S(2)}) %collective-permute-start.7) | collective-permute-done | bytes 786464 | tf_op jit(solution)/shard_map/ppermute | solution.py:211
  82.3 20.3 %shard_map.17 = (f32[128,768]{1,0:T(8,128)S(1)}, f32[128,768]{1,0:T(8,128)S(1)}) custom-call(s32[3]{0:T(128)S(1)} %pad_add_fusion.place, f32[4,6,64,128]{3,2,1,0:T(8,128)S(1)} %bitcast.33, f32[4,6,64,128]{3,2,1,0:T(8,128)S(1)} %collective-permute-done.7.far, f32[3,128,128]{2,1,0:T(8,128)S(1)} %bitcast.37, f32[3,128,128]{2,1,0:T(8,128)S(1)} %collective-permute-done.6.far_row), custom_call_target="tpu_custom_call" | custom-call | flops 1 | bytes 1 | tf_op jit(solution)/shard_map/pallas_call | solution.py:273
  102.6 0.0 all-gather.3.cloned.1.call-done
  102.7 1.2 %copy-done = f32[1024,256]{1,0:T(8,128)S(1)} copy-done((f32[1024,256]{1,0:T(8,128)S(1)}, f32[1024,256]{1,0:T(8,128)}, u32[]{:S(2)}) %copy-start) | copy-done | bytes 1048600
  103.9 1.1 %shard_map.18 = f32[128,256]{1,0:T(8,128)S(1)} custom-call(s32[3]{0:T(128)S(1)} %pad_add_fusion.place, f32[128,256]{1,0:T(8,128)S(1)} %bitcast.43, f32[8,128,256]{2,1,0:T(8,128)S(1)} %bitcast.38, f32[128,768]{1,0:T(8,128)S(1)} %get-tuple-element.15.panel, f32[128,768]{1,0:T(8,128)S(1)} %get-tuple-element.16.weights), custom_call_target="tpu_custom_call" | custom-call | tf_op jit(solution)/shard_map/pallas_call | solution.py:282
  105.0 0.7 reshape.31
  (12 shorter events, 0.1 us)
Async XLA Ops:
  8.3 28.8 %all-to-all-start = ((f32[8,4,32,128]{3,2,1,0:T(8,128)}), f32[8,4,32,128]{3,2,1,0:T(8,128)S(1)}, u32[]{:S(2)}, u32[]{:S(2)}) async-start(f32[8,4,32,128]{3,2,1,0:T(8,128)} %broadcast_in_dim.9), calls=%async_computation | async-start | bytes 1048576 | tf_op jit(solution)/shard_map/all_to_all | solution.py:239
  19.2 10.5 %copy-start.1 = (f32[1,128,2,128]{3,2,1,0:T(2,128)S(1)}, f32[1,128,2,128]{3,2,1,0:T(2,128)}, u32[]{:S(2)}) copy-start(f32[1,128,2,128]{3,2,1,0:T(2,128)} %param.1) | copy-start | bytes 393220
  19.2 7.2 %collective-permute-start = (f32[128,256]{1,0:T(8,128)S(1)}, f32[128,256]{1,0:T(8,128)S(1)}, u32[]{:S(2)}, u32[]{:S(2)}) collective-permute-start(f32[128,256]{1,0:T(8,128)S(1)} %bitcast.40), channel_id=1, source_target_pairs={{0,384},{1,385},{2,386},{3,387},{4,388},{5,389},{6,390},{7,391},{8... | collective-permute-start | bytes 393224 | tf_op jit(solution)/shard_map/ppermute | solution.py:211
  23.7 3.2 %collective-permute-start.1 = (f32[128,256]{1,0:T(8,128)S(1)}, f32[128,256]{1,0:T(8,128)S(1)}, u32[]{:S(2)}, u32[]{:S(2)}) collective-permute-start(f32[128,256]{1,0:T(8,128)S(1)} %bitcast.41), channel_id=1, source_target_pairs={{0,256},{1,257},{2,258},{3,259},{4,260},{5,261},{6,262},{7,263},{8... | collective-permute-start | bytes 393224 | tf_op jit(solution)/shard_map/ppermute | solution.py:211
  25.0 4.6 %collective-permute-start.2 = (f32[128,256]{1,0:T(8,128)S(1)}, f32[128,256]{1,0:T(8,128)S(1)}, u32[]{:S(2)}, u32[]{:S(2)}) collective-permute-start(f32[128,256]{1,0:T(8,128)S(1)} %bitcast.42), channel_id=1, source_target_pairs={{0,128},{1,129},{2,130},{3,131},{4,132},{5,133},{6,134},{7,135},{8... | collective-permute-start | bytes 393224 | tf_op jit(solution)/shard_map/ppermute | solution.py:211
  37.2 7.0 %collective-permute-start.3 = (f32[64,128]{1,0:T(8,128)S(1)}, f32[64,128]{1,0:T(8,128)S(1)}, u32[]{:S(2)}, u32[]{:S(2)}) collective-permute-start(f32[64,128]{1,0:T(8,128)S(1)} %get-tuple-element.19), channel_id=1, source_target_pairs={{0,384},{1,385},{2,386},{3,387},{4,388},{5,389},{6,390},{7,391},{8... | collective-permute-start | bytes 98312 | tf_op jit(solution)/shard_map/ppermute | solution.py:211
  41.6 2.6 %collective-permute-start.4 = (f32[64,128]{1,0:T(8,128)S(1)}, f32[64,128]{1,0:T(8,128)S(1)}, u32[]{:S(2)}, u32[]{:S(2)}) collective-permute-start(f32[64,128]{1,0:T(8,128)S(1)} %get-tuple-element.18), channel_id=1, source_target_pairs={{0,256},{1,257},{2,258},{3,259},{4,260},{5,261},{6,262},{7,263},{8... | collective-permute-start | bytes 98312 | tf_op jit(solution)/shard_map/ppermute | solution.py:211
  42.9 2.3 %collective-permute-start.5 = (f32[64,128]{1,0:T(8,128)S(1)}, f32[64,128]{1,0:T(8,128)S(1)}, u32[]{:S(2)}, u32[]{:S(2)}) collective-permute-start(f32[64,128]{1,0:T(8,128)S(1)} %get-tuple-element.17), channel_id=1, source_target_pairs={{0,128},{1,129},{2,130},{3,131},{4,132},{5,133},{6,134},{7,135},{8... | collective-permute-start | bytes 98312 | tf_op jit(solution)/shard_map/ppermute | solution.py:211
  46.0 16.6 %all-to-all-start.1 = ((f32[8,2,32,128]{3,2,1,0:T(8,128)}), f32[8,2,32,128]{3,2,1,0:T(8,128)S(1)}, u32[]{:S(2)}, u32[]{:S(2)}) async-start(f32[8,2,32,128]{3,2,1,0:T(8,128)} %broadcast_in_dim.10), calls=%async_computation.1 | async-start | bytes 524288 | tf_op jit(solution)/shard_map/all_to_all | solution.py:239
  52.8 49.9 %all-gather.3.cloned.1.call-start = ((), (), s32[]{:S(2)}) async-start(), calls=%async_computation.3 | async-start | bytes 1179648 | tf_op jit(solution)/shard_map/all_gather | solution.py:253
  53.5 9.1 %collective-permute-start.6 = (f32[3,128,128]{2,1,0:T(8,128)S(1)}, f32[3,128,128]{2,1,0:T(8,128)S(1)}, u32[]{:S(2)}, u32[]{:S(2)}) collective-permute-start(f32[3,128,128]{2,1,0:T(8,128)S(1)} %bitcast.36), channel_id=1, source_target_pairs={{0,1},{1,0},{2,3},{3,2},{4,5},{5,4},{6,7},{7,6},{8,9},{9,8},{10,11... | collective-permute-start | bytes 589832 | tf_op jit(solution)/shard_map/ppermute | solution.py:211
  73.5 8.9 %collective-permute-start.7 = (f32[4,6,64,128]{3,2,1,0:T(8,128)S(1)}, f32[4,6,64,128]{3,2,1,0:T(8,128)S(1)}, u32[]{:S(2)}, u32[]{:S(2)}) collective-permute-start(f32[4,6,64,128]{3,2,1,0:T(8,128)S(1)} %bitcast.32), channel_id=1, source_target_pairs={{0,1},{1,0},{2,3},{3,2},{4,5},{5,4},{6,7},{7,6},{8,9},{9,8},{10,11... | collective-permute-start | bytes 2359304 | tf_op jit(solution)/shard_map/ppermute | solution.py:211
  102.7 1.2 %copy-start = (f32[1024,256]{1,0:T(8,128)S(1)}, f32[1024,256]{1,0:T(8,128)}, u32[]{:S(2)}) copy-start(f32[1024,256]{1,0:T(8,128)} %all-gather.3.cloned.1.call-done) | copy-start | bytes 3145732
Sparse Core Ops, SparseCore 0:
  55.7 33.1 all-gather.2
